TPU v7x, 32 devices: a whole 2x2x4 slice. The times are simulated.
32 devices in a mesh: dp: 4 (over x, core), fsdp: 8 (over z, y).
Axes of the slice: x: 2, y: 2, z: 4, core: 2. Of those that a mesh axis runs over, the one named last changes fastest.
Arguments:
- tokens: bfloat16 [128, 128, 1024], P(('dp', 'fsdp')), may hold values from -6 to 6
- seq_counts: int32 [32], P(('dp', 'fsdp')), may hold values from 1 to 4, as said below
- segments: int32 [128, 128], P(('dp', 'fsdp')), may hold values from 0 to 31, as said below
- positions: int32 [128, 128], P(('dp', 'fsdp')), may hold values from 0 to 2428, as said below
- norm_first: bfloat16 [1024], P(('dp', 'fsdp')), may hold values from 0.5 to 1.5
- query_weight: bfloat16 [1024, 1024], P(('dp', 'fsdp')), may hold values from -0.25 to 0.25
- key_weight: bfloat16 [1024, 1024], P(('dp', 'fsdp')), may hold values from -0.1875 to 0.1875
- value_weight: bfloat16 [1024, 1024], P(('dp', 'fsdp')), may hold values from -0.1875 to 0.1875
- output_weight: bfloat16 [1024, 1024], P(('dp', 'fsdp')), may hold values from -0.75 to 0.75
- norm_second: bfloat16 [1024], P(('dp', 'fsdp')), may hold values from 0.5 to 1.5
- gate_weight: bfloat16 [1024, 2816], P(('dp', 'fsdp')), may hold values from -0.1875 to 0.1875
- up_weight: bfloat16 [1024, 2816], P(('dp', 'fsdp')), may hold values from -0.1875 to 0.1875
- down_weight: bfloat16 [2816, 1024], P(('dp', 'fsdp')), may hold values from -0.109375 to 0.109375
- out_cotangent: bfloat16 [128, 128, 1024], P(('dp', 'fsdp')), may hold values from -6 to 6
- value_cotangent: bfloat16 [128, 128, 1024], P(('dp', 'fsdp')), may hold values from -6 to 6
Outputs:
- block_output: bfloat16 [128, 128, 1024], P(('dp', 'fsdp'))
- first_values: bfloat16 [128, 128, 1024], P(('dp', 'fsdp'))
- token_grad: bfloat16 [128, 128, 1024], P(('dp', 'fsdp'))
- norm_first_grad: float32 [1024], P(('dp', 'fsdp'))
- query_grad: float32 [1024, 1024], P(('dp', 'fsdp'))
- key_grad: float32 [1024, 1024], P(('dp', 'fsdp'))
- value_grad: float32 [1024, 1024], P(('dp', 'fsdp'))
- output_grad: float32 [1024, 1024], P(('dp', 'fsdp'))
- norm_second_grad: float32 [1024], P(('dp', 'fsdp'))
- gate_grad: float32 [1024, 2816], P(('dp', 'fsdp'))
- up_grad: float32 [1024, 2816], P(('dp', 'fsdp'))
- down_grad: float32 [2816, 1024], P(('dp', 'fsdp'))
Inputs may be any that keep to these rules, and one draw needn't show every extreme that they name: `seq_counts`: slots 0 to count - 1 of a device's 4 hold live sequences, the others are padding; some device holds 4 and some device 1. `segments`: starts at 0 in every sequence and rises by one at each new document's first token; documents begin only at token indices that are multiples of 4. `positions`: within a document rises by 1 to 3 from one token to the next; a document's first token has a position below 2048.
All inputs are finite; a program needn't handle non-finite values.
Results may differ from a plain program's by a relative error of at most 0.014.
Values may be sent and summed in bfloat16 or wider, within the bound.
A program may use at most 256 MiB of HBM per device.

v0:
```python
import math

import jax
import jax.numpy as jnp
from jax import lax
from jax.sharding import PartitionSpec as P

HD = 64


eps = 1e-06


def rms_scale(values_in):
    return lax.rsqrt(jnp.mean(values_in * values_in, axis=-1, keepdims=True) + eps)


def rotate_table(positions):
    freq_index = jnp.arange(HD // 2, dtype=jnp.float32)
    inverse = jnp.exp(freq_index * (-2.0 * math.log(10000.0) / HD))
    angles = positions.astype(jnp.float32)[..., None] * inverse
    return (jnp.cos(angles), jnp.sin(angles))


def apply_rotary(values_in, cosine, sines):
    half_dim = values_in.shape[-1] // 2
    first_half = values_in[..., :half_dim]
    second_half = values_in[..., half_dim:]
    cosine = cosine[..., None, :]
    sines = sines[..., None, :]
    return jnp.concatenate(
        [first_half * cosine - second_half * sines, second_half * cosine + first_half * sines],
        axis=-1,
    )


def matmul(left_arg, right_arg):
    return jnp.dot(left_arg, right_arg, preferred_element_type=jnp.float32)


def stack_groups(values_in):
    row_count, model_width = values_in.shape
    return values_in.reshape(row_count, model_width // (4 * HD), 4 * HD).transpose(1, 0, 2)


def unstack_groups(values_in):
    group_count, row_count, group_width = values_in.shape
    return values_in.transpose(1, 0, 2).reshape(row_count, group_count * group_width)


def head_scores(query_grp, key_grp, allowed):
    row_count = query_grp.shape[0]
    query_heads = query_grp.reshape(row_count, 4, HD)
    key_heads = key_grp.reshape(row_count, 4, HD)
    scores = jnp.einsum(
        "qhe,khe->hqk", query_heads, key_heads, preferred_element_type=jnp.float32
    ) * HD ** (-0.5)
    return jnp.where(allowed[None], scores, -1e30)


def norm_back(grad_normed, inputs_f, scale_rows, gain_row):
    gain_term = jnp.sum(grad_normed * inputs_f * scale_rows, axis=0)
    scaled = grad_normed * gain_row
    grad_inputs = scale_rows * (
        scaled
        - inputs_f * scale_rows * scale_rows * jnp.mean(scaled * inputs_f, axis=-1, keepdims=True)
    )
    return (grad_inputs, gain_term)


def shards(
    tokens,
    seq_counts,
    segments,
    positions,
    norm_first,
    query_weight,
    key_weight,
    value_weight,
    output_weight,
    norm_second,
    gate_weight,
    up_weight,
    down_weight,
    out_cotangent,
    value_cotangent,
):
    slot_count, seq_length, model_width = tokens.shape
    row_count = slot_count * seq_length
    head_count = model_width // HD
    attention_set = (
        lax.all_gather(norm_first, ("dp", "fsdp"), axis=0, tiled=True),
        lax.all_gather(query_weight, ("dp", "fsdp"), axis=0, tiled=True),
        lax.all_gather(key_weight, ("dp", "fsdp"), axis=0, tiled=True),
        lax.all_gather(value_weight, ("dp", "fsdp"), axis=0, tiled=True),
        lax.all_gather(output_weight, ("dp", "fsdp"), axis=0, tiled=True),
    )
    feedforward_set = (
        lax.all_gather(norm_second, ("dp", "fsdp"), axis=0, tiled=True),
        lax.all_gather(gate_weight, ("dp", "fsdp"), axis=0, tiled=True),
        lax.all_gather(up_weight, ("dp", "fsdp"), axis=0, tiled=True),
        lax.all_gather(down_weight, ("dp", "fsdp"), axis=0, tiled=True),
    )
    gain_one, query_full, key_full, value_full, output_full = attention_set
    gain_two, gate_full, up_full, down_full = feedforward_set
    row_index = jnp.arange(row_count, dtype=jnp.int32)
    slot_index = row_index // seq_length
    live_rows = (slot_index < seq_counts[0]).astype(jnp.float32)[:, None]
    flat_segments = segments.reshape(row_count)
    allowed = (
        (slot_index[:, None] == slot_index[None, :])
        & (flat_segments[:, None] == flat_segments[None, :])
        & (row_index[:, None] >= row_index[None, :])
    )
    inputs_f = tokens.reshape(row_count, model_width).astype(jnp.float32)
    scale_one = rms_scale(inputs_f)
    normed = (inputs_f * scale_one * gain_one.astype(jnp.float32)).astype(jnp.bfloat16)
    cosine, sines = rotate_table(positions.reshape(row_count))

    def rotated(values_in, turn_sign):
        turned = apply_rotary(
            values_in.reshape(row_count, head_count, HD), cosine, turn_sign * sines
        )
        return turned.reshape(row_count, model_width).astype(jnp.bfloat16)

    query_rot = rotated(matmul(normed, query_full), 1.0)
    key_rot = rotated(matmul(normed, key_full), 1.0)
    value_low = matmul(normed, value_full).astype(jnp.bfloat16)

    def attend_group(operands):
        query_grp, key_grp, value_grp = operands
        scores = head_scores(query_grp, key_grp, allowed)
        row_max = jnp.max(scores, axis=-1, keepdims=True)
        log_total = row_max + jnp.log(jnp.sum(jnp.exp(scores - row_max), axis=-1, keepdims=True))
        probs_low = jnp.exp(scores - log_total).astype(jnp.bfloat16)
        value_heads = value_grp.reshape(row_count, 4, HD)
        mixed_heads = jnp.einsum(
            "hqk,khe->qhe", probs_low, value_heads, preferred_element_type=jnp.float32
        )
        return (mixed_heads.reshape(row_count, 4 * HD), log_total)

    query_groups = stack_groups(query_rot)
    key_groups = stack_groups(key_rot)
    value_groups = stack_groups(value_low)
    mixed_groups, log_totals = lax.map(attend_group, (query_groups, key_groups, value_groups))
    mixed_low = unstack_groups(mixed_groups).astype(jnp.bfloat16)
    middle = inputs_f + matmul(mixed_low, output_full)
    scale_two = rms_scale(middle)
    normed_two = (middle * scale_two * gain_two.astype(jnp.float32)).astype(jnp.bfloat16)
    gate_pre = matmul(normed_two, gate_full)
    upward = matmul(normed_two, up_full)
    sigmoid_gate = jax.nn.sigmoid(gate_pre)
    silu_gate = gate_pre * sigmoid_gate
    hidden = (silu_gate * upward).astype(jnp.bfloat16)
    block_out = (live_rows * (middle + matmul(hidden, down_full))).astype(jnp.bfloat16)
    first_values = (live_rows * value_low.astype(jnp.float32)).astype(jnp.bfloat16)
    attention_back = (
        lax.all_gather(norm_first, ("dp", "fsdp"), axis=0, tiled=True),
        lax.all_gather(query_weight, ("dp", "fsdp"), axis=0, tiled=True),
        lax.all_gather(key_weight, ("dp", "fsdp"), axis=0, tiled=True),
        lax.all_gather(value_weight, ("dp", "fsdp"), axis=0, tiled=True),
        lax.all_gather(output_weight, ("dp", "fsdp"), axis=0, tiled=True),
    )
    feedforward_back = (
        lax.all_gather(norm_second, ("dp", "fsdp"), axis=0, tiled=True),
        lax.all_gather(gate_weight, ("dp", "fsdp"), axis=0, tiled=True),
        lax.all_gather(up_weight, ("dp", "fsdp"), axis=0, tiled=True),
        lax.all_gather(down_weight, ("dp", "fsdp"), axis=0, tiled=True),
    )
    gain_one_back, query_back, key_back, value_back, output_back = attention_back
    gain_two_back, gate_back, up_back, down_back = feedforward_back
    grad_y = live_rows * out_cotangent.reshape(row_count, model_width).astype(jnp.float32)
    grad_branch = grad_y.astype(jnp.bfloat16)
    down_term = jnp.einsum("rf,rd->fd", hidden, grad_branch, preferred_element_type=jnp.float32)
    grad_hidden = jnp.einsum(
        "rd,fd->rf", grad_branch, down_back, preferred_element_type=jnp.float32
    )
    grad_gate = (
        grad_hidden * upward * sigmoid_gate * (1.0 + gate_pre * (1.0 - sigmoid_gate))
    ).astype(jnp.bfloat16)
    grad_up = (grad_hidden * silu_gate).astype(jnp.bfloat16)
    gate_term = jnp.einsum("rd,rf->df", normed_two, grad_gate, preferred_element_type=jnp.float32)
    up_term = jnp.einsum("rd,rf->df", normed_two, grad_up, preferred_element_type=jnp.float32)
    grad_normed_two = jnp.einsum(
        "rf,df->rd", grad_gate, gate_back, preferred_element_type=jnp.float32
    ) + jnp.einsum("rf,df->rd", grad_up, up_back, preferred_element_type=jnp.float32)
    grad_middle_norm, gain_two_term = norm_back(
        grad_normed_two, middle, scale_two, gain_two_back.astype(jnp.float32)
    )
    grad_middle = grad_y + grad_middle_norm
    feedforward_grads = (
        lax.psum_scatter(gain_two_term, ("dp", "fsdp"), scatter_dimension=0, tiled=True),
        lax.psum_scatter(gate_term, ("dp", "fsdp"), scatter_dimension=0, tiled=True),
        lax.psum_scatter(up_term, ("dp", "fsdp"), scatter_dimension=0, tiled=True),
        lax.psum_scatter(down_term, ("dp", "fsdp"), scatter_dimension=0, tiled=True),
    )
    grad_attended = grad_middle.astype(jnp.bfloat16)
    output_term = jnp.einsum(
        "rd,re->de", mixed_low, grad_attended, preferred_element_type=jnp.float32
    )
    grad_mixed = jnp.einsum(
        "re,de->rd", grad_attended, output_back, preferred_element_type=jnp.float32
    ).astype(jnp.bfloat16)

    def attend_back(operands):
        query_grp, key_grp, value_grp, grad_grp, log_total = operands
        scores = head_scores(query_grp, key_grp, allowed)
        probs_full = jnp.exp(scores - log_total)
        probs_low = probs_full.astype(jnp.bfloat16)
        grad_heads = grad_grp.reshape(row_count, 4, HD)
        value_heads = value_grp.reshape(row_count, 4, HD)
        query_heads = query_grp.reshape(row_count, 4, HD)
        key_heads = key_grp.reshape(row_count, 4, HD)
        grad_probs = jnp.einsum(
            "qhe,khe->hqk", grad_heads, value_heads, preferred_element_type=jnp.float32
        )
        row_term = jnp.sum(probs_full * grad_probs, axis=-1, keepdims=True)
        grad_scores = (probs_full * (grad_probs - row_term)).astype(jnp.bfloat16)
        score_scale = HD ** (-0.5)
        grad_query = (
            jnp.einsum("hqk,khe->qhe", grad_scores, key_heads, preferred_element_type=jnp.float32)
            * score_scale
        )
        grad_key = (
            jnp.einsum("hqk,qhe->khe", grad_scores, query_heads, preferred_element_type=jnp.float32)
            * score_scale
        )
        grad_value = jnp.einsum(
            "hqk,qhe->khe", probs_low, grad_heads, preferred_element_type=jnp.float32
        )
        group_width = 4 * HD
        return (
            grad_query.reshape(row_count, group_width),
            grad_key.reshape(row_count, group_width),
            grad_value.reshape(row_count, group_width),
        )

    grad_q_groups, grad_k_groups, grad_v_groups = lax.map(
        attend_back, (query_groups, key_groups, value_groups, stack_groups(grad_mixed), log_totals)
    )
    grad_query = rotated(unstack_groups(grad_q_groups), -1.0)
    grad_key = rotated(unstack_groups(grad_k_groups), -1.0)
    grad_value = (
        unstack_groups(grad_v_groups)
        + live_rows * value_cotangent.reshape(row_count, model_width).astype(jnp.float32)
    ).astype(jnp.bfloat16)
    query_term = jnp.einsum("rd,re->de", normed, grad_query, preferred_element_type=jnp.float32)
    key_term = jnp.einsum("rd,re->de", normed, grad_key, preferred_element_type=jnp.float32)
    value_term = jnp.einsum("rd,re->de", normed, grad_value, preferred_element_type=jnp.float32)
    grad_normed = jnp.einsum(
        "re,de->rd", grad_query, query_back, preferred_element_type=jnp.float32
    )
    grad_normed = grad_normed + jnp.einsum(
        "re,de->rd", grad_key, key_back, preferred_element_type=jnp.float32
    )
    grad_normed = grad_normed + jnp.einsum(
        "re,de->rd", grad_value, value_back, preferred_element_type=jnp.float32
    )
    grad_inputs_norm, gain_one_term = norm_back(
        grad_normed, inputs_f, scale_one, gain_one_back.astype(jnp.float32)
    )
    token_grad = (grad_middle + grad_inputs_norm).astype(jnp.bfloat16).reshape(tokens.shape)
    attention_grads = (
        lax.psum_scatter(gain_one_term, ("dp", "fsdp"), scatter_dimension=0, tiled=True),
        lax.psum_scatter(query_term, ("dp", "fsdp"), scatter_dimension=0, tiled=True),
        lax.psum_scatter(key_term, ("dp", "fsdp"), scatter_dimension=0, tiled=True),
        lax.psum_scatter(value_term, ("dp", "fsdp"), scatter_dimension=0, tiled=True),
        lax.psum_scatter(output_term, ("dp", "fsdp"), scatter_dimension=0, tiled=True),
    )
    return (
        block_out.reshape(tokens.shape),
        first_values.reshape(tokens.shape),
        token_grad,
        attention_grads[0],
        attention_grads[1],
        attention_grads[2],
        attention_grads[3],
        attention_grads[4],
        feedforward_grads[0],
        feedforward_grads[1],
        feedforward_grads[2],
        feedforward_grads[3],
    )


def solution(mesh):
    in_specs = (
        P(("dp", "fsdp"), None, None),
        P(("dp", "fsdp")),
        P(("dp", "fsdp"), None),
        P(("dp", "fsdp"), None),
        P(("dp", "fsdp")),
        P(("dp", "fsdp"), None),
        P(("dp", "fsdp"), None),
        P(("dp", "fsdp"), None),
        P(("dp", "fsdp"), None),
        P(("dp", "fsdp")),
        P(("dp", "fsdp"), None),
        P(("dp", "fsdp"), None),
        P(("dp", "fsdp"), None),
        P(("dp", "fsdp"), None, None),
        P(("dp", "fsdp"), None, None),
    )
    out_specs = (
        P(("dp", "fsdp"), None, None),
        P(("dp", "fsdp"), None, None),
        P(("dp", "fsdp"), None, None),
        P(("dp", "fsdp")),
        P(("dp", "fsdp"), None),
        P(("dp", "fsdp"), None),
        P(("dp", "fsdp"), None),
        P(("dp", "fsdp"), None),
        P(("dp", "fsdp")),
        P(("dp", "fsdp"), None),
        P(("dp", "fsdp"), None),
        P(("dp", "fsdp"), None),
    )
    return jax.shard_map(shards, mesh=mesh, in_specs=in_specs, out_specs=out_specs, check_vma=False)
```

profile of v0, /device:TPU:0, one launch (start us, length us, event | category | flops | bytes accessed | tf_op | source)
XLA Modules:
  0.0 1883.6 jit_solution(4212626097791277289)
XLA Ops:
  13.8 42.1 %all-reduce.5 = (bf16[1024]{0:T(1024)(128)(2,1)S(1)}, bf16[1024]{0:T(1024)(128)(2,1)S(1)}) all-reduce(bf16[1024]{0:T(1024)(128)(2,1)S(1)} %dynamic-update-slice, bf16[1024]{0:T(1024)(128)(2,1)S(1)} %dynamic-update-slice.1), channel_id=1, replica_groups=mesh['dp'=4,'fsdp'=8] {'dp','fsdp'}, use_global_device_ids=true, to_apply=%add | all-reduce | flops 2048 | bytes 8192
  61.0 9.3 all-gather.10.cloned.1.call-done
  70.4 4.0 copy.42
  74.4 4.3 fusion.45
  78.7 50.1 %all-gather.8.cloned.1.call-done = bf16[1024,1024]{1,0:T(8,128)(2,1)} async-done(((bf16[32,1024]{1,0:T(8,128)(2,1)}), bf16[1024,1024]{1,0:T(8,128)(2,1)}) %all-gather.8.cloned.1.call-update) | async-done | bytes 2097168 | tf_op jit(solution)/shard_map/all_gather | solution.py:95
  128.8 4.1 convolution_convert_fusion.1
  132.9 54.3 %all-gather.12.cloned.1.call-done = bf16[1024,1024]{1,0:T(8,128)(2,1)} async-done(((bf16[32,1024]{1,0:T(8,128)(2,1)}), bf16[1024,1024]{1,0:T(8,128)(2,1)}) %all-gather.12.cloned.1.call-update) | async-done | bytes 2097168 | tf_op jit(solution)/shard_map/all_gather | solution.py:94
  187.2 4.0 copy.43
  192.6 3.3 fusion.46
  198.2 18.1 while.30
  216.4 29.1 %all-gather.14.cloned.1.call-done = bf16[1024,1024]{1,0:T(8,128)(2,1)} async-done(((bf16[32,1024]{1,0:T(8,128)(2,1)}), bf16[1024,1024]{1,0:T(8,128)(2,1)}) %all-gather.14.cloned.1.call-update) | async-done | bytes 2097168 | tf_op jit(solution)/shard_map/all_gather | solution.py:96
  245.4 3.3 multiply_reduce_fusion.3
  249.0 65.3 %all-gather.16.cloned.1.call-done = bf16[1024,2816]{1,0:T(8,128)(2,1)} async-done(((bf16[32,2816]{1,0:T(8,128)(2,1)}), bf16[1024,2816]{1,0:T(8,128)(2,1)}) %all-gather.16.cloned.1.call-update) | async-done | bytes 5767184 | tf_op jit(solution)/shard_map/all_gather | solution.py:100
  314.3 7.8 fusion.47
  322.1 61.2 %all-gather.18.cloned.1.call-done = bf16[1024,2816]{1,0:T(8,128)(2,1)} async-done(((bf16[32,2816]{1,0:T(8,128)(2,1)}), bf16[1024,2816]{1,0:T(8,128)(2,1)}) %all-gather.18.cloned.1.call-update) | async-done | bytes 5767184 | tf_op jit(solution)/shard_map/all_gather | solution.py:101
  383.3 8.6 fusion.48
  392.0 60.5 %all-gather.20.cloned.1.call-done = bf16[2816,1024]{1,0:T(8,128)(2,1)} async-done(((bf16[88,1024]{1,0:T(8,128)(2,1)}), bf16[2816,1024]{1,0:T(8,128)(2,1)}) %all-gather.20.cloned.1.call-update) | async-done | bytes 5767184 | tf_op jit(solution)/shard_map/all_gather | solution.py:102
  452.5 10.8 multiply_convert_fusion.1
  463.3 7.3 fusion.49
  470.7 3.5 multiply_reduce_fusion.1
  474.2 2.5 fusion.18
  476.7 2.3 convolution_convert_fusion
  482.1 1.6 broadcast.243.clone
  483.7 55.4 %while.31 = (s32[]{:T(128)}, f32[4,512,256]{1,2,0:T(8,128)}, f32[4,512,256]{1,2,0:T(8,128)}, f32[4,512,256]{1,2,0:T(8,128)}, bf16[4,512,256]{1,2,0:T(8,128)(2,1)...) while((s32[]{:T(128)}, f32[4,512,256]{1,2,0:T(8,128)}, ...), condition=%wide.region_9.10_spmd.clone.clone, body=%wide.region_7.9_spmd.clone.sunk.clone | while | flops 688388096 | bytes 41219200 | solution.py:238
  539.1 3.8 multiply_subtract_fusion
  544.6 3.3 fusion.53
  549.1 3.2 fusion.37
  554.6 3.3 fusion.52
  559.1 1.9 reshape.381
  561.0 2.9 copy.54
  563.9 2.9 fusion.22
  566.8 3.3 fusion.54
  571.3 7.8 fusion.55
  579.2 7.8 fusion.56
  588.2 8.0 fusion.57
  596.3 3.0 copy.53
  599.3 3.0 fusion.51
  606.9 3.0 fusion.36
  609.9 41.4 %all-reduce.4 = (f32[1024]{0:T(1024)S(1)}, f32[1024]{0:T(1024)S(1)}) all-reduce(f32[1024]{0:T(1024)S(1)} %get-tuple-element.157, f32[1024]{0:T(1024)S(1)} %get-tuple-element.155), channel_id=2, replica_groups=mesh['dp'=4,'fsdp'=8] {'dp','fsdp'}, use_global_device_ids=true, to_apply=%region_12.13.clone | all-reduce | flops 2048 | bytes 16384
  652.5 3.3 fusion.30
  655.8 6.8 multiply_convert_fusion.5
  662.6 28.7 %reduce-scatter.10.cloned.1.call-done = f32[32,1024]{1,0:T(8,128)} async-done(((f32[1024,1024]{1,0:T(8,128)}), f32[32,1024]{1,0:T(8,128)}) %reduce-scatter.10.cloned.1.call-update) | async-done | bytes 131088 | tf_op jit(solution)/shard_map/reduce_scatter | solution.py:266
  691.3 144.3 %reduce-scatter.14.cloned.1.call-done = f32[32,1024]{1,0:T(8,128)} async-done(((f32[1024,1024]{1,0:T(8,128)}), f32[32,1024]{1,0:T(8,128)}) %reduce-scatter.14.cloned.1.call-update) | async-done | bytes 131088 | tf_op jit(solution)/shard_map/reduce_scatter | solution.py:268
  835.6 144.8 %reduce-scatter.8.cloned.1.call-done = f32[32,1024]{1,0:T(8,128)} async-done(((f32[1024,1024]{1,0:T(8,128)}), f32[32,1024]{1,0:T(8,128)}) %reduce-scatter.8.cloned.1.call-update) | async-done | bytes 131088 | tf_op jit(solution)/shard_map/reduce_scatter | solution.py:265
  980.4 144.5 %reduce-scatter.12.cloned.1.call-done = f32[32,1024]{1,0:T(8,128)} async-done(((f32[1024,1024]{1,0:T(8,128)}), f32[32,1024]{1,0:T(8,128)}) %reduce-scatter.12.cloned.1.call-update) | async-done | bytes 131088 | tf_op jit(solution)/shard_map/reduce_scatter | solution.py:267
  1124.8 249.8 %reduce-scatter.16.cloned.1.call-done = f32[32,2816]{1,0:T(8,128)} async-done(((f32[1024,2816]{1,0:T(8,128)}), f32[32,2816]{1,0:T(8,128)}) %reduce-scatter.16.cloned.1.call-update) | async-done | bytes 360464 | tf_op jit(solution)/shard_map/reduce_scatter | solution.py:193
  1374.6 251.5 %reduce-scatter.18.cloned.1.call-done = f32[32,2816]{1,0:T(8,128)} async-done(((f32[1024,2816]{1,0:T(8,128)}), f32[32,2816]{1,0:T(8,128)}) %reduce-scatter.18.cloned.1.call-update) | async-done | bytes 360464 | tf_op jit(solution)/shard_map/reduce_scatter | solution.py:194
  1626.1 250.6 %reduce-scatter.20.cloned.1.call-done = f32[88,1024]{1,0:T(8,128)} async-done(((f32[2816,1024]{1,0:T(8,128)}), f32[88,1024]{1,0:T(8,128)}) %reduce-scatter.20.cloned.1.call-update) | async-done | bytes 360464 | tf_op jit(solution)/shard_map/reduce_scatter | solution.py:195
  (232 shorter events, 94.6 us)
Async XLA Ops:
  7.2 48.7 %copy-start = (bf16[4,128,1024]{2,1,0:T(8,128)(2,1)S(1)}, bf16[4,128,1024]{2,1,0:T(8,128)(2,1)}, u32[]{:S(2)}) copy-start(bf16[4,128,1024]{2,1,0:T(8,128)(2,1)} %param.19) | copy-start | bytes 3145732
  7.2 49.0 %copy-start.36 = (s32[4,128]{1,0:T(4,128)S(1)}, s32[4,128]{1,0:T(4,128)}, u32[]{:S(2)}) copy-start(s32[4,128]{1,0:T(4,128)} %param.22) | copy-start | bytes 6148
  7.2 63.2 %all-gather.10.cloned.1.call-start = ((), (), s32[]{:S(2)}) async-start(), calls=%async_computation.8 | async-start | bytes 2162688 | tf_op jit(solution)/shard_map/all_gather | solution.py:93
  7.9 120.8 %all-gather.8.cloned.1.call-start = ((), (), s32[]{:S(2)}) async-start(), calls=%async_computation.7 | async-start | bytes 2162688 | tf_op jit(solution)/shard_map/all_gather | solution.py:95
  8.7 178.5 %all-gather.12.cloned.1.call-start = ((), (), s32[]{:S(2)}) async-start(), calls=%async_computation.9 | async-start | bytes 2162688 | tf_op jit(solution)/shard_map/all_gather | solution.py:94
  9.4 236.0 %all-gather.14.cloned.1.call-start = ((), (), s32[]{:S(2)}) async-start(), calls=%async_computation.10 | async-start | bytes 2162688 | tf_op jit(solution)/shard_map/all_gather | solution.py:96
  10.0 304.3 %all-gather.16.cloned.1.call-start = ((), (), s32[]{:S(2)}) async-start(), calls=%async_computation.11 | async-start | bytes 5947392 | tf_op jit(solution)/shard_map/all_gather | solution.py:100
  10.6 372.8 %all-gather.18.cloned.1.call-start = ((), (), s32[]{:S(2)}) async-start(), calls=%async_computation.12 | async-start | bytes 5947392 | tf_op jit(solution)/shard_map/all_gather | solution.py:101
  11.2 441.4 %all-gather.20.cloned.1.call-start = ((), (), s32[]{:S(2)}) async-start(), calls=%async_computation.13 | async-start | bytes 5947392 | tf_op jit(solution)/shard_map/all_gather | solution.py:102
  11.9 679.4 %reduce-scatter.10.cloned.1.call-start = ((), (), s32[]{:S(2)}) async-start(), calls=%async_computation.15 | async-start | bytes 4325376 | tf_op jit(solution)/shard_map/reduce_scatter | solution.py:266
  55.9 1.6 copy-start.32
  56.2 2.6 copy-start.34
  56.2 3.6 copy-start.8
  70.4 4.1 copy-start.21
  192.6 3.4 copy-start.13
  196.7 1.5 copy-start.31
  216.3 29.1 %copy-start.4 = (bf16[4,512,256]{1,2,0:T(8,128)(2,1)}, bf16[4,512,256]{1,2,0:T(8,128)(2,1)S(1)}, u32[]{:S(2)}) copy-start(bf16[4,512,256]{1,2,0:T(8,128)(2,1)S(1)} %get-tuple-element.500) | copy-start | bytes 3145732
  216.4 29.1 %copy-start.5 = (bf16[4,512,256]{1,2,0:T(8,128)(2,1)}, bf16[4,512,256]{1,2,0:T(8,128)(2,1)S(1)}, u32[]{:S(2)}) copy-start(bf16[4,512,256]{1,2,0:T(8,128)(2,1)S(1)} %get-tuple-element.104) | copy-start | bytes 3145732
  248.7 222.0 %copy-start.2 = (f32[512,1024]{1,0:T(8,128)}, f32[512,1024]{1,0:T(8,128)S(1)}, u32[]{:S(2)}) copy-start(f32[512,1024]{1,0:T(8,128)S(1)} %get-tuple-element.234) | copy-start | bytes 6291460
  249.0 65.3 %copy-start.25 = (bf16[512,1024]{1,0:T(8,128)(2,1)}, bf16[512,1024]{1,0:T(8,128)(2,1)S(1)}, u32[]{:S(2)}) copy-start(bf16[512,1024]{1,0:T(8,128)(2,1)S(1)} %multiply_convert_fusion.6) | copy-start | bytes 3145732
  322.1 130.4 %copy-start.19 = (bf16[512,1024]{1,0:T(8,128)(2,1)S(1)}, bf16[512,1024]{1,0:T(8,128)(2,1)}, u32[]{:S(2)}) copy-start(bf16[512,1024]{1,0:T(8,128)(2,1)} %fusion.19) | copy-start | bytes 3145732
  463.3 7.4 copy-start.39
  463.3 7.4 copy-start.38
  463.3 7.4 copy-start.37
  470.7 3.5 copy-start.9
  474.2 2.5 copy-start.15
  543.0 1.6 copy-start.22
  547.9 287.7 %reduce-scatter.14.cloned.1.call-start = ((), (), s32[]{:S(2)}) async-start(), calls=%async_computation.17 | async-start | bytes 4325376 | tf_op jit(solution)/shard_map/reduce_scatter | solution.py:268
  552.3 428.0 %reduce-scatter.8.cloned.1.call-start = ((), (), s32[]{:S(2)}) async-start(), calls=%async_computation.14 | async-start | bytes 4325376 | tf_op jit(solution)/shard_map/reduce_scatter | solution.py:265
  552.4 2.2 copy-start.23
  557.9 567.0 %reduce-scatter.12.cloned.1.call-start = ((), (), s32[]{:S(2)}) async-start(), calls=%async_computation.16 | async-start | bytes 4325376 | tf_op jit(solution)/shard_map/reduce_scatter | solution.py:267
  563.9 2.9 copy-start.24
  570.1 804.6 %reduce-scatter.16.cloned.1.call-start = ((), (), s32[]{:S(2)}) async-start(), calls=%async_computation.18 | async-start | bytes 11894784 | tf_op jit(solution)/shard_map/reduce_scatter | solution.py:193
  579.1 1047.0 %reduce-scatter.18.cloned.1.call-start = ((), (), s32[]{:S(2)}) async-start(), calls=%async_computation.19 | async-start | bytes 11894784 | tf_op jit(solution)/shard_map/reduce_scatter | solution.py:194
  587.0 1.2 copy-start.20
  587.0 1289.7 %reduce-scatter.20.cloned.1.call-start = ((), (), s32[]{:S(2)}) async-start(), calls=%async_computation.20 | async-start | bytes 11894784 | tf_op jit(solution)/shard_map/reduce_scatter | solution.py:195
  596.3 3.0 copy-start.28
  599.3 3.1 copy-start.14
  599.3 3.1 copy-start.30
  602.4 1.6 copy-start.7
  602.4 1.9 copy-start.11
  602.4 2.2 copy-start.12
  604.6 1.5 copy-start.1
  604.6 2.3 copy-start.18
  604.6 2.3 copy-start.33
  604.6 2.3 copy-start.35
  652.5 3.4 copy-start.3
  652.5 3.4 copy-start.40
  (7 other events, 7.9 us)
Sparse Core Ops, SparseCore 0:
  11.0 59.3 all-gather.9
  73.3 55.3 all-gather.7
  131.7 55.3 all-gather.11
  190.0 55.3 all-gather.13
  248.2 66.0 all-gather.15
  317.1 66.2 all-gather.17
  386.3 66.2 all-gather.19
  548.0 143.2 reduce-scatter.9
  694.1 141.4 reduce-scatter.13
  838.3 142.0 reduce-scatter.7
  983.2 141.5 reduce-scatter.11
  1127.6 246.9 reduce-scatter.15
  1377.5 248.5 reduce-scatter.17
  1628.9 247.7 reduce-scatter.19
where the time goes:
time: 1890 us; the launch traced here: 1880 us
  waiting for transfers between devices  1550 us (82%)
  matrix products  134 us (7%)
  blocking collectives  83.5 us (4%)
  local copies, waits for them, and re-layouts  58.8 us (3%)
  other arithmetic  31.8 us (2%)
    reduce_scatter x1, waiting for transfers between devices, shards(): lax.psum_scatter(up_term, ('dp', 'fsdp'), scatter_dimension=0, tiled=True)  252 us
    reduce_scatter x1, waiting for transfers between devices, shards(): lax.psum_scatter(down_term, ('dp', 'fsdp'), scatter_dimension=0, tiled=True)  251 us
    reduce_scatter x1, waiting for transfers between devices, shards(): lax.psum_scatter(gate_term, ('dp', 'fsdp'), scatter_dimension=0, tiled=True)  250 us
    reduce_scatter x1, waiting for transfers between devices, shards(): lax.psum_scatter(query_term, ('dp', 'fsdp'), scatter_dimension=0, tiled=T...  145 us
    reduce_scatter x1, waiting for transfers between devices, shards(): lax.psum_scatter(value_term, ('dp', 'fsdp'), scatter_dimension=0, tiled=T...  144 us
    reduce_scatter x1, waiting for transfers between devices, shards(): lax.psum_scatter(output_term, ('dp', 'fsdp'), scatter_dimension=0, tiled=...  144 us
    unnamed x2, blocking collectives  83.5 us
    all_gather x1, waiting for transfers between devices, shards(): lax.all_gather(gate_weight, ('dp', 'fsdp'), axis=0, tiled=True)  65.3 us
  transfers between devices with their start and end apart: 14, of which 14 were waited for; matrix products, arithmetic and copies ran while one was open for 7% of the time, Pallas kernels for 0%

commit v1 on v0

--- a/solution.py
+++ b/solution.py
@@ -3,12 +3,433 @@
 import jax
 import jax.numpy as jnp
 from jax import lax
+from jax.experimental import pallas as pl
+from jax.experimental.pallas import tpu as pltpu
 from jax.sharding import PartitionSpec as P
 
 HD = 64
-
+MESH = pl.DeviceIdType.MESH
+BOTH = ("dp", "fsdp")
 
 eps = 1e-06
+
+
+class Place:
+    def __init__(self, depth):
+        dp, fsdp = lax.axis_index("dp"), lax.axis_index("fsdp")
+        self.x, self.c = dp // 2, dp % 2
+        self.z, self.y = fsdp // 2, fsdp % 2
+        self.depth = depth
+
+    def at(self, x, c, z, y):
+        return (x * 2 + c, z * 2 + y)
+
+    def across_x(self):
+        return self.at(1 - self.x, self.c, self.z, self.y)
+
+    def across_y(self):
+        return self.at(self.x, self.c, self.z, 1 - self.y)
+
+    def sibling(self):
+        return self.at(self.x, 1 - self.c, self.z, self.y)
+
+    def above(self):
+        return self.at(self.x, self.c, self.z + 1, self.y)
+
+    def below(self):
+        return self.at(self.x, self.c, self.z - 1, self.y)
+
+    def greet(self):
+        barrier = pltpu.get_barrier_semaphore()
+
+        def call(who):
+            pl.semaphore_signal(barrier, inc=1, device_id=who, device_id_type=MESH)
+
+        call(self.across_x())
+        call(self.across_y())
+        call(self.sibling())
+        not_top = self.z < self.depth - 1
+        not_low = self.z > 0
+        pl.when(not_top)(lambda: call(self.above()))
+        pl.when(not_low)(lambda: call(self.below()))
+        peers = 3 + not_top.astype(jnp.int32) + not_low.astype(jnp.int32)
+        pl.semaphore_wait(barrier, peers)
+
+
+def remote(src, dst, send_sem, recv_sem, who):
+    return pltpu.make_async_remote_copy(
+        src_ref=src,
+        dst_ref=dst,
+        send_sem=send_sem,
+        recv_sem=recv_sem,
+        device_id=who,
+        device_id_type=MESH,
+    )
+
+
+class Gather:
+    def __init__(self, place, own, full, sems, order):
+        self.p, self.own, self.full, self.sems, self.order = place, own, full, sems, order
+        self.wide = full.shape[-1]
+
+    def shard(self, x, y, z):
+        return self.full.at[x, self.p.c, z, y]
+
+    def zunit(self, z):
+        if self.order == "zr":
+            return self.full.at[self.p.x, self.p.c, z, self.p.y]
+        return self.full.at[:, self.p.c, z]
+
+    def runit(self, x, y, half=None):
+        if self.order == "zr":
+            if half is None:
+                return self.full.at[x, self.p.c, :, y]
+            count = self.p.depth // 2
+            return self.full.at[x, self.p.c, half * count : (half + 1) * count, y]
+        if half is None:
+            return self.full.at[x, self.p.c, self.p.z, y]
+        count = self.wide // 2
+        return self.full.at[x, self.p.c, self.p.z, y, :, half * count : (half + 1) * count]
+
+    def copy(self, ref, slot, who, src=None):
+        return remote(ref if src is None else src, ref, self.sems.at[0, slot], self.sems.at[1, slot], who)
+
+    def up(self, unit, src=None):
+        return self.copy(self.zunit(unit), unit, self.p.above(), src)
+
+    def down(self, unit, src=None):
+        return self.copy(self.zunit(unit), self.p.depth + unit, self.p.below(), src)
+
+    def place_own(self):
+        p = self.p
+        self.local = pltpu.make_async_copy(self.own, self.shard(p.x, p.y, p.z), self.sems.at[0, 22])
+        self.local.start()
+
+    def z_step(self, step):
+        p = self.p
+        top, low = p.depth - 1, 0
+        src = self.own if (step == 0 and self.order == "zr") else None
+
+        def from_below():
+            if step > 0:
+                self.up(p.z - step).wait_recv()
+            pl.when(p.z < top)(lambda: self.up(p.z - step, src).start())
+
+        def from_above():
+            if step > 0:
+                self.down(p.z + step).wait_recv()
+            pl.when(p.z > low)(lambda: self.down(p.z + step, src).start())
+
+        pl.when(p.z - step >= low)(from_below)
+        pl.when(p.z + step <= top)(from_above)
+
+    def ring_first(self):
+        p, base = self.p, 2 * self.p.depth
+        mine = self.runit(p.x, p.y)
+        src = self.own if self.order == "rz" else None
+        self.copy(mine, base, p.across_x(), src).start()
+        self.copy(mine, base + 1, p.across_y(), src).start()
+
+    def ring_second(self):
+        p, base = self.p, 2 * self.p.depth
+        from_x, from_y = self.runit(1 - p.x, p.y), self.runit(p.x, 1 - p.y)
+        self.copy(from_x, base, p.across_x()).wait_recv()
+        self.copy(self.runit(1 - p.x, p.y, 0), base + 2, p.across_y()).start()
+        self.copy(from_y, base + 1, p.across_y()).wait_recv()
+        self.copy(self.runit(p.x, 1 - p.y, 1), base + 3, p.across_x()).start()
+
+    def ring_last(self):
+        p, base = self.p, 2 * self.p.depth
+        self.copy(self.runit(1 - p.x, 1 - p.y, 0), base + 2, p.across_y()).wait_recv()
+        self.copy(self.runit(1 - p.x, 1 - p.y, 1), base + 3, p.across_x()).wait_recv()
+
+    def give(self, ref, slot):
+        self.copy(ref, 2 * self.p.depth + 4 + slot, self.p.sibling()).start()
+
+    def sib_ref(self, kind):
+        p, c = self.p, 1 - self.p.c
+        if self.order == "zr":
+            x = (p.x, 1 - p.x, p.x, 1 - p.x)[kind]
+            y = (p.y, p.y, 1 - p.y, 1 - p.y)[kind]
+            return self.full.at[x, c, :, y]
+        return self.full.at[:, c, kind]
+
+    def my_ref(self, kind):
+        p, c = self.p, self.p.c
+        if self.order == "zr":
+            x = (p.x, 1 - p.x, p.x, 1 - p.x)[kind]
+            y = (p.y, p.y, 1 - p.y, 1 - p.y)[kind]
+            return self.full.at[x, c, :, y]
+        return self.full.at[:, c, kind]
+
+    def steps(self):
+        p = self.p
+        if self.order == "zr":
+            return [
+                lambda: (self.place_own(), self.z_step(0)),
+                lambda: self.z_step(1),
+                lambda: self.z_step(2),
+                lambda: (self.z_step(3), self.local.wait(), self.ring_first(), self.give(self.my_ref(0), 0)),
+                lambda: (self.ring_second(), self.give(self.my_ref(1), 1), self.give(self.my_ref(2), 2)),
+                lambda: (self.ring_last(), self.give(self.my_ref(3), 3)),
+                lambda: self.finish(),
+            ]
+
+        def pass_on(step):
+            def low():
+                self.give(self.full.at[:, p.c, p.z - step], p.z - step)
+
+            def high():
+                self.give(self.full.at[:, p.c, p.z + step], p.z + step)
+
+            pl.when(p.z - step >= 0)(low)
+            if step > 0:
+                pl.when(p.z + step <= p.depth - 1)(high)
+
+        return [
+            lambda: (self.place_own(), self.ring_first()),
+            lambda: self.ring_second(),
+            lambda: (self.ring_last(), self.local.wait(), self.z_step(0), pass_on(0)),
+            lambda: (self.z_step(1), pass_on(1)),
+            lambda: (self.z_step(2), pass_on(2)),
+            lambda: (self.z_step(3), pass_on(3)),
+            lambda: self.finish(),
+        ]
+
+    def finish(self):
+        p, base = self.p, 2 * self.p.depth
+        for kind in range(4):
+            self.copy(self.sib_ref(kind), base + 4 + kind, p.sibling()).wait_recv()
+        top = p.depth - 1
+        for unit in range(p.depth):
+            pl.when((p.z < top) & (unit <= p.z))(lambda unit=unit: self.up(unit).wait_send())
+            pl.when((p.z > 0) & (unit >= p.z))(lambda unit=unit: self.down(unit).wait_send())
+        self.copy(self.runit(p.x, p.y), base, p.across_x()).wait_send()
+        self.copy(self.runit(p.x, p.y), base + 1, p.across_y()).wait_send()
+        self.copy(self.runit(1 - p.x, p.y, 0), base + 2, p.across_y()).wait_send()
+        self.copy(self.runit(p.x, 1 - p.y, 1), base + 3, p.across_x()).wait_send()
+        for kind in range(4):
+            self.copy(self.my_ref(kind), base + 4 + kind, p.sibling()).wait_send()
+
+
+GATHER_ORDERS = ("zr",) * 8
+
+
+def gather_kernel(depth, count, *refs):
+    owns, fulls, sems = refs[:count], refs[count : 2 * count], refs[2 * count]
+    place = Place(depth)
+    place.greet()
+    jobs = [
+        Gather(place, owns[i], fulls[i], sems.at[i], GATHER_ORDERS[i]).steps() for i in range(count)
+    ]
+    stages = len(jobs[0])
+    for tick in range(count + stages - 1):
+        for stage in reversed(range(stages)):
+            if 0 <= tick - stage < count:
+                jobs[tick - stage][stage]()
+
+
+def gather_all(mesh, shards_in):
+    depth = mesh.shape["fsdp"] // 2
+    count = len(shards_in)
+    return pl.pallas_call(
+        lambda *refs: gather_kernel(depth, count, *refs),
+        out_shape=tuple(
+            jax.ShapeDtypeStruct((2, 2, depth, 2) + s.shape, s.dtype) for s in shards_in
+        ),
+        in_specs=[pl.BlockSpec(memory_space=pl.ANY)] * count,
+        out_specs=tuple([pl.BlockSpec(memory_space=pl.ANY)] * count),
+        scratch_shapes=[pltpu.SemaphoreType.DMA((count, 2, 24))],
+        compiler_params=pltpu.CompilerParams(collective_id=1, has_side_effects=True),
+        name="gather_weights",
+    )(*shards_in)
+
+
+class Reduce:
+    def __init__(self, place, part, out, bufs, sems):
+        self.p, self.part, self.out, self.sems = place, part, out, sems
+        self.acc, self.sib, self.ring1, self.ring2, self.zed = bufs
+
+    def copy(self, src, dst, slot, who):
+        return remote(src, dst, self.sems.at[0, slot], self.sems.at[1, slot], who)
+
+    def sib_copy(self):
+        p = self.p
+        return self.copy(self.part.at[:, 1 - p.c], self.sib, 0, p.sibling())
+
+    def own_copy(self):
+        return pltpu.make_async_copy(self.part.at[:, self.p.c], self.acc, self.sems.at[0, 1])
+
+    def start(self):
+        self.sib_copy().start()
+        self.own_copy().start()
+
+    def half1(self):
+        p, half = self.p, self.p.depth // 2
+        by_x = self.copy(self.acc.at[1 - p.x, :half, 1 - p.y], self.ring1.at[0], 2, p.across_x())
+        by_y = self.copy(self.acc.at[1 - p.x, half:, 1 - p.y], self.ring1.at[1], 3, p.across_y())
+        return by_x, by_y
+
+    def half2(self):
+        p = self.p
+        to_x = self.copy(self.acc.at[1 - p.x, :, p.y], self.ring2.at[0], 4, p.across_x())
+        to_y = self.copy(self.acc.at[p.x, :, 1 - p.y], self.ring2.at[1], 5, p.across_y())
+        return to_x, to_y
+
+    def after_sibling(self):
+        self.own_copy().wait()
+        self.sib_copy().wait_recv()
+        p = self.p
+        first = (1 - p.x, 1 - p.y)
+        self.add_bundle(*first, self.sib)
+        for cp in self.half1():
+            cp.start()
+        for x, y in ((1 - p.x, p.y), (p.x, 1 - p.y), (p.x, p.y)):
+            self.add_bundle(x, y, self.sib)
+
+    def add_bundle(self, x, y, other):
+        for z in range(self.p.depth):
+            self.acc[x, z, y] = self.acc[x, z, y] + other[x, z, y]
+
+    def after_half(self):
+        p, half = self.p, self.p.depth // 2
+        by_x, by_y = self.half1()
+        to_x, to_y = self.half2()
+        by_x.wait_recv()
+        for z in range(half):
+            self.acc[p.x, z, 1 - p.y] = self.acc[p.x, z, 1 - p.y] + self.ring1[0, z]
+        to_y.start()
+        by_y.wait_recv()
+        for z in range(half):
+            self.acc[1 - p.x, half + z, p.y] = self.acc[1 - p.x, half + z, p.y] + self.ring1[1, z]
+        to_x.start()
+
+    def up(self, unit):
+        p = self.p
+        return self.copy(self.acc.at[p.x, unit, p.y], self.zed.at[0, unit], 6 + unit, p.above())
+
+    def down(self, unit):
+        p = self.p
+        return self.copy(self.acc.at[p.x, unit, p.y], self.zed.at[1, unit], 6 + p.depth + unit, p.below())
+
+    def after_ring(self):
+        p = self.p
+        to_x, to_y = self.half2()
+        to_x.wait_recv()
+        to_y.wait_recv()
+        for z in range(p.depth):
+            both = self.ring2[0, z].astype(jnp.float32) + self.ring2[1, z].astype(jnp.float32)
+            mine = self.acc[p.x, z, p.y]
+            self.acc[p.x, z, p.y] = (mine.astype(jnp.float32) + both).astype(mine.dtype)
+        self.z_step(0)
+
+    def z_step(self, step):
+        p = self.p
+        top = p.depth - 1
+
+        def upward():
+            if step > 0:
+                for unit in range(step, p.depth):
+                    self.up(unit).wait_recv()
+                for unit in range(step + 1, p.depth):
+                    self.acc[p.x, unit, p.y] = self.acc[p.x, unit, p.y] + self.zed[0, unit]
+            if step < top:
+                for unit in range(step + 1, p.depth):
+                    self.up(unit).start()
+
+        def downward():
+            if step > 0:
+                for unit in range(0, p.depth - step):
+                    self.down(unit).wait_recv()
+                for unit in range(0, p.depth - step - 1):
+                    self.acc[p.x, unit, p.y] = self.acc[p.x, unit, p.y] + self.zed[1, unit]
+            if step < top:
+                for unit in range(0, p.depth - step - 1):
+                    self.down(unit).start()
+
+        pl.when(p.z == step)(upward)
+        pl.when(p.z == top - step)(downward)
+
+    def finish(self):
+        p, top = self.p, self.p.depth - 1
+        mine = self.acc[p.x, p.z, p.y].astype(jnp.float32)
+
+        @pl.when(p.z == 0)
+        def _():
+            self.out[...] = mine + self.zed[1, p.z].astype(jnp.float32)
+
+        @pl.when(p.z == top)
+        def _():
+            self.out[...] = mine + self.zed[0, p.z].astype(jnp.float32)
+
+        @pl.when((p.z > 0) & (p.z < top))
+        def _():
+            self.out[...] = mine + (
+                self.zed[0, p.z].astype(jnp.float32) + self.zed[1, p.z].astype(jnp.float32)
+            )
+
+        self.sib_copy().wait_send()
+        for cp in self.half1() + self.half2():
+            cp.wait_send()
+        for unit in range(p.depth):
+            if unit > 0:
+                pl.when(p.z < unit)(lambda unit=unit: self.up(unit).wait_send())
+            if unit < top:
+                pl.when(p.z > unit)(lambda unit=unit: self.down(unit).wait_send())
+
+    def steps(self):
+        return [
+            self.start,
+            self.after_sibling,
+            self.after_half,
+            self.after_ring,
+            lambda: self.z_step(1),
+            lambda: self.z_step(2),
+            lambda: (self.z_step(3), self.finish()),
+        ]
+
+
+def reduce_kernel(depth, count, *refs):
+    parts, outs = refs[:count], refs[count : 2 * count]
+    bufs = refs[2 * count : 2 * count + 5 * count]
+    sems = refs[-1]
+    place = Place(depth)
+    place.greet()
+    jobs = [
+        Reduce(place, parts[i], outs[i], bufs[5 * i : 5 * i + 5], sems.at[i]).steps()
+        for i in range(count)
+    ]
+    stages = len(jobs[0])
+    for tick in range(count + stages - 1):
+        for stage in reversed(range(stages)):
+            if 0 <= tick - stage < count:
+                jobs[tick - stage][stage]()
+
+
+def reduce_all(mesh, parts):
+    depth = mesh.shape["fsdp"] // 2
+    count = len(parts)
+    bufs = []
+    for part in parts:
+        block, kind = part.shape[4:], part.dtype
+        bufs += [
+            pltpu.VMEM((2, depth, 2) + block, kind),
+            pltpu.VMEM((2, depth, 2) + block, kind),
+            pltpu.VMEM((2, depth // 2) + block, kind),
+            pltpu.VMEM((2, depth) + block, kind),
+            pltpu.VMEM((2, depth) + block, kind),
+        ]
+    return pl.pallas_call(
+        lambda *refs: reduce_kernel(depth, count, *refs),
+        out_shape=tuple(jax.ShapeDtypeStruct(p.shape[4:], jnp.float32) for p in parts),
+        in_specs=[pl.BlockSpec(memory_space=pl.ANY)] * count,
+        out_specs=tuple([pl.BlockSpec(memory_space=pltpu.VMEM)] * count),
+        scratch_shapes=bufs + [pltpu.SemaphoreType.DMA((count, 2, 16))],
+        compiler_params=pltpu.CompilerParams(
+            collective_id=2, has_side_effects=True, vmem_limit_bytes=60 * 2**20
+        ),
+        name="reduce_grads",
+    )(*parts)
 
 
 def rms_scale(values_in):
@@ -68,7 +489,9 @@
     return (grad_inputs, gain_term)
 
 
-def shards(
+def layer(
+    gather_set,
+    reduce_set,
     tokens,
     seq_counts,
     segments,
@@ -88,21 +511,19 @@
     slot_count, seq_length, model_width = tokens.shape
     row_count = slot_count * seq_length
     head_count = model_width // HD
-    attention_set = (
-        lax.all_gather(norm_first, ("dp", "fsdp"), axis=0, tiled=True),
-        lax.all_gather(query_weight, ("dp", "fsdp"), axis=0, tiled=True),
-        lax.all_gather(key_weight, ("dp", "fsdp"), axis=0, tiled=True),
-        lax.all_gather(value_weight, ("dp", "fsdp"), axis=0, tiled=True),
-        lax.all_gather(output_weight, ("dp", "fsdp"), axis=0, tiled=True),
-    )
-    feedforward_set = (
-        lax.all_gather(norm_second, ("dp", "fsdp"), axis=0, tiled=True),
-        lax.all_gather(gate_weight, ("dp", "fsdp"), axis=0, tiled=True),
-        lax.all_gather(up_weight, ("dp", "fsdp"), axis=0, tiled=True),
-        lax.all_gather(down_weight, ("dp", "fsdp"), axis=0, tiled=True),
-    )
-    gain_one, query_full, key_full, value_full, output_full = attention_set
-    gain_two, gate_full, up_full, down_full = feedforward_set
+    weights = gather_set(
+        norm_first,
+        norm_second,
+        query_weight,
+        key_weight,
+        value_weight,
+        output_weight,
+        gate_weight,
+        up_weight,
+        down_weight,
+    )
+    gain_one, gain_two, query_full, key_full, value_full, output_full = weights[:6]
+    gate_full, up_full, down_full = weights[6:]
     row_index = jnp.arange(row_count, dtype=jnp.int32)
     slot_index = row_index // seq_length
     live_rows = (slot_index < seq_counts[0]).astype(jnp.float32)[:, None]
@@ -154,26 +575,11 @@
     hidden = (silu_gate * upward).astype(jnp.bfloat16)
     block_out = (live_rows * (middle + matmul(hidden, down_full))).astype(jnp.bfloat16)
     first_values = (live_rows * value_low.astype(jnp.float32)).astype(jnp.bfloat16)
-    attention_back = (
-        lax.all_gather(norm_first, ("dp", "fsdp"), axis=0, tiled=True),
-        lax.all_gather(query_weight, ("dp", "fsdp"), axis=0, tiled=True),
-        lax.all_gather(key_weight, ("dp", "fsdp"), axis=0, tiled=True),
-        lax.all_gather(value_weight, ("dp", "fsdp"), axis=0, tiled=True),
-        lax.all_gather(output_weight, ("dp", "fsdp"), axis=0, tiled=True),
-    )
-    feedforward_back = (
-        lax.all_gather(norm_second, ("dp", "fsdp"), axis=0, tiled=True),
-        lax.all_gather(gate_weight, ("dp", "fsdp"), axis=0, tiled=True),
-        lax.all_gather(up_weight, ("dp", "fsdp"), axis=0, tiled=True),
-        lax.all_gather(down_weight, ("dp", "fsdp"), axis=0, tiled=True),
-    )
-    gain_one_back, query_back, key_back, value_back, output_back = attention_back
-    gain_two_back, gate_back, up_back, down_back = feedforward_back
     grad_y = live_rows * out_cotangent.reshape(row_count, model_width).astype(jnp.float32)
     grad_branch = grad_y.astype(jnp.bfloat16)
     down_term = jnp.einsum("rf,rd->fd", hidden, grad_branch, preferred_element_type=jnp.float32)
     grad_hidden = jnp.einsum(
-        "rd,fd->rf", grad_branch, down_back, preferred_element_type=jnp.float32
+        "rd,fd->rf", grad_branch, down_full, preferred_element_type=jnp.float32
     )
     grad_gate = (
         grad_hidden * upward * sigmoid_gate * (1.0 + gate_pre * (1.0 - sigmoid_gate))
@@ -182,24 +588,18 @@
     gate_term = jnp.einsum("rd,rf->df", normed_two, grad_gate, preferred_element_type=jnp.float32)
     up_term = jnp.einsum("rd,rf->df", normed_two, grad_up, preferred_element_type=jnp.float32)
     grad_normed_two = jnp.einsum(
-        "rf,df->rd", grad_gate, gate_back, preferred_element_type=jnp.float32
-    ) + jnp.einsum("rf,df->rd", grad_up, up_back, preferred_element_type=jnp.float32)
+        "rf,df->rd", grad_gate, gate_full, preferred_element_type=jnp.float32
+    ) + jnp.einsum("rf,df->rd", grad_up, up_full, preferred_element_type=jnp.float32)
     grad_middle_norm, gain_two_term = norm_back(
-        grad_normed_two, middle, scale_two, gain_two_back.astype(jnp.float32)
+        grad_normed_two, middle, scale_two, gain_two.astype(jnp.float32)
     )
     grad_middle = grad_y + grad_middle_norm
-    feedforward_grads = (
-        lax.psum_scatter(gain_two_term, ("dp", "fsdp"), scatter_dimension=0, tiled=True),
-        lax.psum_scatter(gate_term, ("dp", "fsdp"), scatter_dimension=0, tiled=True),
-        lax.psum_scatter(up_term, ("dp", "fsdp"), scatter_dimension=0, tiled=True),
-        lax.psum_scatter(down_term, ("dp", "fsdp"), scatter_dimension=0, tiled=True),
-    )
     grad_attended = grad_middle.astype(jnp.bfloat16)
     output_term = jnp.einsum(
         "rd,re->de", mixed_low, grad_attended, preferred_element_type=jnp.float32
     )
     grad_mixed = jnp.einsum(
-        "re,de->rd", grad_attended, output_back, preferred_element_type=jnp.float32
+        "re,de->rd", grad_attended, output_full, preferred_element_type=jnp.float32
     ).astype(jnp.bfloat16)
 
     def attend_back(operands):
@@ -248,39 +648,91 @@
     key_term = jnp.einsum("rd,re->de", normed, grad_key, preferred_element_type=jnp.float32)
     value_term = jnp.einsum("rd,re->de", normed, grad_value, preferred_element_type=jnp.float32)
     grad_normed = jnp.einsum(
-        "re,de->rd", grad_query, query_back, preferred_element_type=jnp.float32
+        "re,de->rd", grad_query, query_full, preferred_element_type=jnp.float32
     )
     grad_normed = grad_normed + jnp.einsum(
-        "re,de->rd", grad_key, key_back, preferred_element_type=jnp.float32
+        "re,de->rd", grad_key, key_full, preferred_element_type=jnp.float32
     )
     grad_normed = grad_normed + jnp.einsum(
-        "re,de->rd", grad_value, value_back, preferred_element_type=jnp.float32
+        "re,de->rd", grad_value, value_full, preferred_element_type=jnp.float32
     )
     grad_inputs_norm, gain_one_term = norm_back(
-        grad_normed, inputs_f, scale_one, gain_one_back.astype(jnp.float32)
+        grad_normed, inputs_f, scale_one, gain_one.astype(jnp.float32)
     )
     token_grad = (grad_middle + grad_inputs_norm).astype(jnp.bfloat16).reshape(tokens.shape)
-    attention_grads = (
-        lax.psum_scatter(gain_one_term, ("dp", "fsdp"), scatter_dimension=0, tiled=True),
-        lax.psum_scatter(query_term, ("dp", "fsdp"), scatter_dimension=0, tiled=True),
-        lax.psum_scatter(key_term, ("dp", "fsdp"), scatter_dimension=0, tiled=True),
-        lax.psum_scatter(value_term, ("dp", "fsdp"), scatter_dimension=0, tiled=True),
-        lax.psum_scatter(output_term, ("dp", "fsdp"), scatter_dimension=0, tiled=True),
+    grads = reduce_set(
+        gain_one_term,
+        gain_two_term,
+        query_term,
+        key_term,
+        value_term,
+        output_term,
+        gate_term,
+        up_term,
+        down_term,
     )
     return (
         block_out.reshape(tokens.shape),
         first_values.reshape(tokens.shape),
         token_grad,
-        attention_grads[0],
-        attention_grads[1],
-        attention_grads[2],
-        attention_grads[3],
-        attention_grads[4],
-        feedforward_grads[0],
-        feedforward_grads[1],
-        feedforward_grads[2],
-        feedforward_grads[3],
-    )
+        grads[0],
+        grads[2],
+        grads[3],
+        grads[4],
+        grads[5],
+        grads[1],
+        grads[6],
+        grads[7],
+        grads[8],
+    )
+
+
+def plain_gather(*shards_in):
+    return tuple(lax.all_gather(s, BOTH, axis=0, tiled=True) for s in shards_in)
+
+
+def plain_reduce(*terms):
+    return tuple(lax.psum_scatter(t, BOTH, scatter_dimension=0, tiled=True) for t in terms)
+
+
+def linked_gather(mesh):
+    def gather(gain_one, gain_two, *weights):
+        down = weights[-1]
+        rows, wide = down.shape
+        gains = jnp.zeros((8, 128), jnp.float32)
+        gains = gains.at[0, : gain_one.shape[0]].set(gain_one.astype(jnp.float32))
+        gains = gains.at[1, : gain_two.shape[0]].set(gain_two.astype(jnp.float32))
+        down = down.reshape(rows, 2, wide // 2).transpose(1, 0, 2).reshape(2 * rows, wide // 2)
+        fulls = gather_all(mesh, (gains,) + weights[:-1] + (down,))
+        gains_full = fulls[0].reshape(-1, 8, 128)
+        ones = gains_full[:, 0, : gain_one.shape[0]].reshape(-1).astype(jnp.bfloat16)
+        twos = gains_full[:, 1, : gain_two.shape[0]].reshape(-1).astype(jnp.bfloat16)
+        whole = [f.reshape(-1, f.shape[-1]) for f in fulls[1:-1]]
+        down = fulls[-1].reshape(-1, 2, rows, wide // 2).transpose(0, 2, 1, 3)
+        return (ones, twos) + tuple(whole) + (down.reshape(-1, wide),)
+
+    return gather
+
+
+def linked_reduce(mesh):
+    lead = (2, 2, mesh.shape["fsdp"] // 2, 2)
+    count = mesh.size
+
+    def reduce(gain_one, gain_two, *terms):
+        each = gain_one.shape[0] // count
+        gains = jnp.zeros((count, 8, 128), jnp.float32)
+        gains = gains.at[:, 0, :each].set(gain_one.reshape(count, each))
+        gains = gains.at[:, 1, :each].set(gain_two.reshape(count, each))
+        low = [t.astype(jnp.bfloat16) for t in terms]
+        parts = [t.reshape(lead + (t.shape[0] // count, t.shape[1])) for t in low[:-1]]
+        rows, wide = low[-1].shape[0] // count, low[-1].shape[1]
+        down = low[-1].reshape(count, rows, 2, wide // 2).transpose(0, 2, 1, 3)
+        down = down.reshape(lead + (2 * rows, wide // 2))
+        outs = reduce_all(mesh, [gains.reshape(lead + (8, 128))] + parts + [down])
+        down = outs[-1].reshape(2, rows, wide // 2).transpose(1, 0, 2).reshape(rows, wide)
+        return (outs[0][0, :each], outs[0][1, :each]) + tuple(outs[1:-1]) + (down,)
+
+    return reduce
 
 
 def solution(mesh):
@@ -315,4 +767,12 @@
         P(("dp", "fsdp"), None),
         P(("dp", "fsdp"), None),
     )
+    if dict(mesh.shape) == {"dp": 4, "fsdp": 8}:
+        sets = (linked_gather(mesh), linked_reduce(mesh))
+    else:
+        sets = (plain_gather, plain_reduce)
+
+    def shards(*args):
+        return layer(*sets, *args)
+
     return jax.shard_map(shards, mesh=mesh, in_specs=in_specs, out_specs=out_specs, check_vma=False)

time: 1890 us -> 517 us (0.27)
  waiting for transfers between devices: 1550 us -> 0 us
  Pallas kernels: 0 us -> 273 us
  blocking collectives: 83.5 us -> 0 us
  local copies, waits for them, and re-layouts: 58.8 us -> 96.9 us
  matrix products: 134 us -> 113 us
    reduce_scatter x7 -> x0, waiting for transfers between devices: 1210 us -> none  [the longest x1 252 us: shards(): lax.psum_scatter(up_term, ('dp', 'fsdp'), scatter_dimension=0, tiled=True)]
    all_gather x7 -> x0, waiting for transfers between devices: 330 us -> none  [the longest x1 65.3 us: shards(): lax.all_gather(gate_weight, ('dp', 'fsdp'), axis=0, tiled=True)]
    pallas_call x0 -> x2, Pallas kernels: none -> 273 us  [the longest x1 137 us: gather_all(): pl.pallas_call(lambda *refs: gather_kernel(depth, count, *refs), out_shap...]
    unnamed x2 -> x0, blocking collectives: 83.5 us -> none
    reshape x1 -> x5, local copies, waits for them, and re-layouts: 3.03 us -> 29.8 us  [the longest x2 17 us: reduce(): down = low[-1].reshape(count, rows, 2, wide // 2).transpose(0, 2, 1, 3)]
  transfers between devices with their start and end apart: 14 -> 0, of which waited for: 14 -> 0; matrix products, arithmetic and copies ran while one was open for 7% -> 0% of each run, Pallas kernels for 0% -> 0%
where the time goes in v1:
time: 517 us; the launch traced here: 512 us
  Pallas kernels  273 us (53%)
  matrix products  113 us (22%)
  local copies, waits for them, and re-layouts  96.9 us (19%)
  other arithmetic  26.9 us (5%)
    pallas_call x1, Pallas kernels, gather_all(): pl.pallas_call(lambda *refs: gather_kernel(depth, count, *refs), out_shap...  137 us
    pallas_call x1, Pallas kernels, reduce_all(): pl.pallas_call(lambda *refs: reduce_kernel(depth, count, *refs), out_shap...  136 us
    dot_general x7, matrix products, matmul(): return jnp.dot(left_arg, right_arg, preferred_element_type=jnp.float32)  29.3 us
    dynamic_slice x24, local copies, waits for them, and re-layouts, layer(): lax.map(attend_group, (query_groups, key_groups, value_groups))  19.6 us
    unnamed x99, local copies, waits for them, and re-layouts  17.1 us
    reshape x2, local copies, waits for them, and re-layouts, reduce(): down = low[-1].reshape(count, rows, 2, wide // 2).transpose(0, 2, 1, 3)  17 us

profile of v1, /device:TPU:0, one launch (start us, length us, event | category | flops | bytes accessed | tf_op | source)
XLA Modules:
  0.0 511.8 jit_solution(1457673589650440916)
XLA Ops:
  3.1 1.6 copy.63
  4.7 136.6 %gather_weights.1 = (f32[2,2,4,2,8,128]{5,4,3,2,1,0:T(8,128)}, bf16[2,2,4,2,32,1024]{5,4,3,2,1,0:T(8,128)(2,1)}, bf16[2,2,4,2,32,1024]{5,4,3,2,1,0:T(8,128)(2,1)...) custom-call(f32[8,128]{1,0:T(8,128)} %copy-done.34, ...), custom_call_target="tpu_custom_call" | custom-call | tf_op jit(solution)/shard_map/gather_weights/pallas_call | solution.py:235
  146.6 4.0 copy.46
  150.6 4.5 fusion.45
  156.1 4.0 copy.45
  160.1 3.0 fusion.44
  165.0 20.5 %while.34 = (s32[]{:T(128)}, bf16[4,512,256]{1,2,0:T(8,128)(2,1)}, f32[4,4,512,1]{2,1,3,0:T(4,128)S(1)}, bf16[4,512,256]{1,2,0:T(8,128)(2,1)S(1)}, bf16[4,512,25...) while((s32[]{:T(128)}, bf16[4,512,256]{1,2,0:T(8,128)(2,1)}, ...), condition=%wide.region_4.5_spmd.clone.clone, body=%wide.region_1.4_spmd.clone.sunk.clone | while | flops 281278464 | bytes 16846956 | solution.py:566
  186.9 3.3 multiply_reduce_fusion.3
  190.5 8.1 %fusion.46 = f32[512,2816]{1,0:T(8,128)} fusion(bf16[512,1024]{1,0:T(8,128)(2,1)S(1)} %multiply_convert_fusion.7, bf16[1024,2816]{1,0:T(8,128)(2,1)} %bitcast.342), kind=kOutput, calls=%fused_computation.136 | convolution fusion | flops 2952790016 | bytes 12582912 | tf_op jit(solution)/shard_map/dot_general | solution.py:459
  198.6 5.0 fusion.47
  204.6 9.5 %copy.47 = bf16[32,2,88,512]{3,1,2,0:T(2,128)(2,1)S(1)} copy(bf16[32,2,88,512]{3,2,1,0:T(8,128)(2,1)S(1)} %bitcast.292) | data formatting | bytes 11534336 | tf_op jit(solution)/shard_map/reshape | solution.py:711
  214.0 1.9 copy.61
  215.9 9.3 %multiply_convert_fusion.1 = (bf16[512,2816]{1,0:T(8,128)(2,1)S(1)}, bf16[512,2816]{1,0:T(8,128)(2,1)}, bf16[512,2816]{1,0:T(8,128)(2,1)S(1)}) fusion(f32[512,2816]{1,0:T(8,128)} %fusion.46, f32[512,2816]{1,0:T(8,128)} %fusion.47, bf16[512,1024]{1,0:T(8,128)(2,1)S(1)} %bitcast.324, bf16[2816,1024]{1,0:T(8,128)(2,1)S(1)} %bitcast.293), kind=kOutput, calls=%fused_computation.38 | convolution fusion | flops 2974416896 | bytes 27000832 | tf_op jit(solution)/shard_map/rd,fd->rf/dot_general | solution.py:581
  225.3 4.2 multiply_convert_fusion.6
  229.5 5.2 %fusion.48 = f32[512,1024]{1,0:T(8,128)S(1)} fusion(bf16[512,2816]{1,0:T(8,128)(2,1)S(1)} %copy-done.40, bf16[1024,2816]{1,0:T(8,128)(2,1)} %bitcast.343), kind=kOutput, calls=%fused_computation.138 | convolution fusion | flops 2952790016 | bytes 10747904 | tf_op jit(solution)/shard_map/rf,df->rd/dot_general | solution.py:590
  234.7 5.7 %multiply_reduce_fusion.1 = (f32[1024]{0:T(1024)S(1)}, f32[512]{0:T(512)S(1)}, f32[512,1024]{1,0:T(8,128)S(1)}) fusion(f32[512,1024]{1,0:T(8,128)S(1)} %get-tuple-element.315, f32[512]{0:T(512)S(1)} %add_rsqrt_fusion, f32[1024]{0:T(1024)S(1)} %reshape.644, f32[512,1024]{1,0:T(8,128)S(1)} %fusion.48, bf16[512,2816]{1,0:T(8,128)(2,1)S(1)} %get-tuple-element.289, ...), kind=kOutput, calls=%fused_computation.67 | convolution fusion | flops 2956458496 | bytes 14954496 | tf_op jit(solution)/shard_map/rf,df->rd/dot_general | solution.py:592
  240.5 3.0 fusion.31
  243.4 3.5 convolution_convert_fusion.7
  246.9 1.3 copy.57
  248.5 1.6 broadcast.332.clone
  250.2 48.0 %while.35 = (s32[]{:T(128)}, f32[4,512,256]{1,2,0:T(8,128)}, f32[4,512,256]{1,2,0:T(8,128)S(1)}, f32[4,512,256]{1,2,0:T(8,128)}, bf16[4,512,256]{1,2,0:T(8,128)(...) while((s32[]{:T(128)}, f32[4,512,256]{1,2,0:T(8,128)}, ...), condition=%wide.region_9.10_spmd.clone.clone, body=%wide.region_7.9_spmd.clone.sunk.clone | while | flops 688388096 | bytes 41218192 | solution.py:638
  255.3 1.5 multiply_reduce_fusion.6
  267.2 1.5 multiply_reduce_fusion.6
  279.1 1.5 multiply_reduce_fusion.6
  291.1 1.5 multiply_reduce_fusion.6
  298.1 3.0 reshape.655
  301.2 2.9 copy.58
  304.1 2.9 fusion.18
  307.8 1.8 copy-done.13
  309.7 1.3 fusion.49
  314.6 2.0 fusion.30
  316.6 1.7 fusion.27
  319.2 4.3 convolution_convert_fusion.6
  323.6 2.7 convolution_convert_fusion.5
  326.3 2.7 convolution_convert_fusion.4
  329.0 2.6 convolution_convert_fusion.3
  331.6 5.1 convolution_convert_fusion.2
  336.7 5.0 convolution_convert_fusion.1
  341.8 5.1 convolution_convert_fusion
  346.8 10.5 %reshape.636 = bf16[32,88,2,512]{3,2,1,0:T(2,128)(2,1)} reshape(bf16[2816,1024]{1,0:T(8,128)(2,1)} %convolution_convert_fusion) | data formatting | bytes 11534336 | tf_op jit(solution)/shard_map/reshape | solution.py:729
  357.3 6.5 %copy.50 = bf16[32,88,2,512]{3,1,2,0:T(8,128)(2,1)} copy(bf16[32,88,2,512]{3,2,1,0:T(2,128)(2,1)} %reshape.636) | data formatting | bytes 11534336 | tf_op jit(solution)/shard_map/reshape | solution.py:729
  363.8 135.9 %reduce_grads.1 = (f32[8,128]{1,0:T(8,128)}, f32[32,1024]{1,0:T(8,128)}, f32[32,1024]{1,0:T(8,128)}, f32[32,1024]{1,0:T(8,128)}, f32[32,1024]{1,0:T(8,128)}, /*i...) custom-call(f32[2,2,4,2,8,128]{5,4,3,2,1,0:T(8,128)} %bitcast.332, ...), custom_call_target="tpu_custom_call" | custom-call | tf_op jit(solution)/shard_map/reduce_grads/pallas_call | solution.py:422
  501.1 1.7 copy.60
  502.8 1.6 copy.100
  504.4 1.6 copy.101
  506.0 1.6 copy.102
  507.5 1.6 copy.103
  509.1 1.7 copy.104
  (216 shorter events, 82.0 us)
Async XLA Ops:
  0.6 141.8 %copy-start = (bf16[4,128,1024]{2,1,0:T(8,128)(2,1)S(1)}, bf16[4,128,1024]{2,1,0:T(8,128)(2,1)}, u32[]{:S(2)}) copy-start(bf16[4,128,1024]{2,1,0:T(8,128)(2,1)} %param.27) | copy-start | bytes 3145732
  3.1 1.6 copy-start.34
  142.4 1.2 copy-start.31
  142.4 2.2 copy-start.14
  143.6 1.0 copy-start.17
  145.9 4.7 copy-start.5
  150.6 4.5 copy-start.35
  156.1 7.1 %copy-start.26 = (f32[512,32]{0,1:T(8,128)}, f32[512,32]{0,1:T(8,128)S(1)}, u32[]{:S(2)}) copy-start(f32[512,32]{0,1:T(8,128)S(1)} %get-tuple-element.310) | copy-start | bytes 196612
  156.1 4.0 copy-start.18
  160.1 3.0 copy-start.10
  163.9 1.1 copy-start.25
  185.5 1.0 copy-start.1
  185.5 1.4 copy-start.2
  190.2 8.4 %slice-start.2 = ((s8[5767168]{0:T(1024)(128)(4,1)}), s8[4194304]{0:T(1024)(128)(4,1)S(1)}, s32[]{:S(2)}) async-start(s8[5767168]{0:T(1024)(128)(4,1)} %bitcast.339), calls=%async_computation.2 | async-start | bytes 8388608
  190.5 8.1 %copy-start.20 = (bf16[512,1024]{1,0:T(8,128)(2,1)}, bf16[512,1024]{1,0:T(8,128)(2,1)S(1)}, u32[]{:S(2)}) copy-start(bf16[512,1024]{1,0:T(8,128)(2,1)S(1)} %multiply_convert_fusion.7) | copy-start | bytes 3145732
  190.5 8.1 %slice-start.3 = ((s8[5767168]{0:T(1024)(128)(4,1)}), s8[1572864]{0:T(1024)(128)(4,1)S(1)}, s32[]{:S(2)}) async-start(s8[5767168]{0:T(1024)(128)(4,1)} %bitcast.339), calls=%async_computation.3 | async-start | bytes 3145728
  198.6 6.0 %slice-start = ((s8[5767168]{0:T(1024)(128)(4,1)}), s8[4194304]{0:T(1024)(128)(4,1)S(1)}, s32[]{:S(2)}) async-start(s8[5767168]{0:T(1024)(128)(4,1)} %bitcast.290), calls=%async_computation | async-start | bytes 8388608
  198.6 5.7 %copy-start.4 = (bf16[4,128,1024]{2,1,0:T(8,128)(2,1)S(1)}, bf16[4,128,1024]{2,1,0:T(8,128)(2,1)}, u32[]{:S(2)}) copy-start(bf16[4,128,1024]{2,1,0:T(8,128)(2,1)} %param.40) | copy-start | bytes 3145732
  198.6 5.9 %slice-start.1 = ((s8[5767168]{0:T(1024)(128)(4,1)}), s8[1572864]{0:T(1024)(128)(4,1)S(1)}, s32[]{:S(2)}) async-start(s8[5767168]{0:T(1024)(128)(4,1)} %bitcast.290), calls=%async_computation.1 | async-start | bytes 3145728
  225.3 4.2 copy-start.38
  225.3 9.4 %copy-start.36 = (bf16[512,2816]{1,0:T(8,128)(2,1)}, bf16[512,2816]{1,0:T(8,128)(2,1)S(1)}, u32[]{:S(2)}) copy-start(bf16[512,2816]{1,0:T(8,128)(2,1)S(1)} %get-tuple-element.289) | copy-start | bytes 8650756
  225.3 4.2 copy-start.40
  234.7 5.8 %copy-start.6 = (bf16[512,1024]{1,0:T(8,128)(2,1)S(1)}, bf16[512,1024]{1,0:T(8,128)(2,1)}, u32[]{:S(2)}) copy-start(bf16[512,1024]{1,0:T(8,128)(2,1)} %copy-done.5) | copy-start | bytes 3145732
  304.1 2.9 copy-start.11
  304.1 2.9 copy-start.27
  304.1 3.0 copy-start.30
  307.0 7.3 %copy-start.8 = (bf16[512,4,256]{0,2,1:T(8,128)(2,1)}, bf16[512,4,256]{0,2,1:T(8,128)(2,1)S(1)}, u32[]{:S(2)}) copy-start(bf16[512,4,256]{0,2,1:T(8,128)(2,1)S(1)} %fusion.18) | copy-start | bytes 3145732
  307.7 2.0 copy-start.13
  307.8 3.2 copy-start.22
  311.0 2.0 copy-start.12
  311.1 1.0 copy-start.23
  313.0 1.6 copy-start.15
  313.0 1.6 copy-start.32
  313.0 1.6 copy-start.33
  314.6 2.0 copy-start.3
  319.2 4.4 copy-start.28
  319.2 4.4 copy-start.19
  319.2 4.3 copy-start.24
  323.6 2.7 copy-start.9
  326.3 2.7 copy-start.7
  329.0 2.6 copy-start.21
  329.0 2.6 copy-start.41
  331.6 5.1 copy-start.37
  336.7 5.0 copy-start.16
  336.7 5.0 copy-start.39
  499.8 11.1 %copy-start.29 = (f32[32,2816]{1,0:T(8,128)S(1)}, f32[32,2816]{1,0:T(8,128)}, u32[]{:S(2)}) copy-start(f32[32,2816]{1,0:T(8,128)} %get-tuple-element.587) | copy-start | bytes 1081348

commit v2 on v1

--- a/solution.py
+++ b/solution.py
@@ -2,6 +2,7 @@
 
 import jax
 import jax.numpy as jnp
+import numpy as np
 from jax import lax
 from jax.experimental import pallas as pl
 from jax.experimental.pallas import tpu as pltpu
@@ -212,37 +213,363 @@
             self.copy(self.my_ref(kind), base + 4 + kind, p.sibling()).wait_send()
 
 
-GATHER_ORDERS = ("zr",) * 8
-
-
-def gather_kernel(depth, count, *refs):
-    owns, fulls, sems = refs[:count], refs[count : 2 * count], refs[2 * count]
+WIDE = 256
+
+
+def iota(shape, dim):
+    return lax.broadcasted_iota(jnp.int32, shape, dim)
+
+
+def to_column(row):
+    n = row.shape[1]
+    eye = iota((n, n), 0) == iota((n, n), 1)
+    return jnp.sum(jnp.where(eye, jnp.broadcast_to(row, (n, n)), 0.0), axis=1, keepdims=True)
+
+
+def dot(a, b, dims=((1,), (0,))):
+    return lax.dot_general(a, b, (dims, ((), ())), preferred_element_type=jnp.float32)
+
+
+def turn(values, cosine, sines):
+    outs = []
+    first = iota((values.shape[0], 128), 1) % HD < HD // 2
+    for g in range(values.shape[1] // 128):
+        part = values[:, g * 128 : (g + 1) * 128]
+        other = jnp.where(
+            first, pltpu.roll(part, 128 - HD // 2, 1), pltpu.roll(part, HD // 2, 1)
+        )
+        outs.append(part * cosine + other * sines)
+    return jnp.concatenate(outs, axis=1)
+
+
+def gain_row(gains, row, each):
+    count = gains.shape[0]
+    rows = gains[:, row, :]
+    whole = jnp.concatenate([rows] * (count * each // 128), axis=1)
+    shape = whole.shape
+    keep = iota(shape, 1) // each == iota(shape, 0)
+    return jnp.sum(jnp.where(keep, whole, 0.0), axis=0, keepdims=True)
+
+
+class Forward:
+    def __init__(self, place, refs):
+        self.p = place
+        self.__dict__.update(refs)
+        self.slots, self.length = self.segments.shape
+        self.rows = self.slots * self.length
+
+    def load(self, name, cols=None):
+        full, dst = getattr(self, name + "_full"), getattr(self, name + "_v")
+        slot = self.load_slots[(name, cols)]
+        if cols is not None:
+            lo, hi = cols
+            full, dst = full.at[:, :, :, :, :, lo:hi], dst.at[:, :, :, :, :, lo:hi]
+        return pltpu.make_async_copy(full, dst, self.load_sems.at[slot])
+
+    def save(self, name):
+        slot = self.save_slots[name]
+        return pltpu.make_async_copy(
+            getattr(self, name + "_v"), getattr(self, name + "_out"), self.save_sems.at[slot]
+        )
+
+    def tables(self):
+        for b in range(self.slots):
+            rows = pl.ds(b * self.length, self.length)
+            angles = to_column(self.positions[b : b + 1, :].astype(jnp.float32)) * self.inverse[...]
+            first = iota(angles.shape, 1) % HD < HD // 2
+            sines = jnp.sin(angles)
+            self.cos_v[rows, :] = jnp.cos(angles)
+            self.sin_v[rows, :] = jnp.where(first, -sines, sines)
+            seg = self.segments[b : b + 1, :].astype(jnp.float32)
+            shape = (self.length, self.length)
+            allowed = (to_column(seg) == seg) & (iota(shape, 0) >= iota(shape, 1))
+            self.bias_v[b] = jnp.where(allowed, 0.0, -1e30)
+        self.save("cos").start()
+        self.save("sin").start()
+
+    def gains(self):
+        pltpu.make_async_copy(self.g_full, self.g_v, self.load_sems.at[0]).start()
+        pltpu.make_async_copy(self.g_full, self.g_v, self.load_sems.at[0]).wait()
+        count = math.prod(self.g_v.shape[:4])
+        gains = self.g_v[...].reshape(count, 8, 128)
+        each = self.width // count
+        self.gain_v[0:1, :] = gain_row(gains, 0, each)
+        self.gain_v[1:2, :] = gain_row(gains, 1, each)
+
+    def norm_one(self):
+        for b in range(self.slots):
+            rows = pl.ds(b * self.length, self.length)
+            inputs = self.tokens[rows, :].astype(jnp.float32)
+            scale = lax.rsqrt(jnp.mean(inputs * inputs, axis=-1, keepdims=True) + eps)
+            normed = (inputs * scale * self.gain_v[0:1, :]).astype(jnp.bfloat16)
+            self.normed_v[rows, :] = normed
+            self.normed_t_v[:, rows] = normed.T
+        self.save("normed_t").start()
+
+    def weight(self, name, cols):
+        w = getattr(self, name + "_v")[:, :, :, :, :, cols]
+        return w.reshape(math.prod(w.shape[:5]), w.shape[5])
+
+    def project(self, name):
+        self.load(name).wait()
+        normed = self.normed_v[...]
+
+        def tile(n, carry):
+            cols = pl.ds(pl.multiple_of(n * WIDE, WIDE), WIDE)
+            got = dot(normed, self.weight(name, cols))
+            if name == "v":
+                low = got.astype(jnp.bfloat16)
+                self.v_low_v[:, cols] = low
+                self.first_v[:, cols] = (self.live_v[...][:, 0:1] * low.astype(jnp.float32)).astype(jnp.bfloat16)
+            else:
+                turned = turn(got, self.cos_v[...], self.sin_v[...])
+                getattr(self, name + "_rot_v")[:, cols] = turned.astype(jnp.bfloat16)
+            return carry
+
+        lax.fori_loop(0, self.width // WIDE, tile, 0)
+        if name == "v":
+            self.save("v_low").start()
+            self.save("first").start()
+        else:
+            self.save(name + "_rot").start()
+
+    def live(self):
+        index = iota((self.rows, 128), 0) // self.length
+        self.live_v[...] = (index < self.counts[0]).astype(jnp.float32)
+
+    def attend(self, b):
+        length = self.length
+        rows = pl.ds(b * length, length)
+
+        def pair(h, carry):
+            cols = pl.ds(pl.multiple_of(h * 128, 128), 128)
+            q, k, v = self.q_rot_v[rows, cols], self.k_rot_v[rows, cols], self.v_low_v[rows, cols]
+            k2, v2 = split_pair(k), split_pair(v)
+            scores = dot(q, k2, ((1,), (1,))) * HD ** (-0.5)
+            bias = self.bias_v[b]
+            probs = []
+            for half in range(2):
+                s = scores[:, half * length : (half + 1) * length] + bias
+                e = jnp.exp(s - jnp.max(s, axis=-1, keepdims=True))
+                probs.append(e * (1.0 / jnp.sum(e, axis=-1, keepdims=True)))
+            probs = jnp.concatenate(probs, axis=1).astype(jnp.bfloat16)
+            self.probs_v[b, h] = probs
+            self.mixed_v[rows, cols] = dot(probs, v2).astype(jnp.bfloat16)
+            return carry
+
+        lax.fori_loop(0, self.width // 128, pair, 0)
+        self.mixed_t_v[:, rows] = self.mixed_v[rows, :].T
+        if b == self.slots - 1:
+            self.save("probs").start()
+            self.save("mixed_t").start()
+
+    def join(self):
+        self.load("o").wait()
+        mixed = self.mixed_v[...]
+
+        def tile(n, carry):
+            cols = pl.ds(pl.multiple_of(n * WIDE, WIDE), WIDE)
+            got = dot(mixed, self.weight("o", cols))
+            self.middle_v[:, cols] = self.tokens[:, cols].astype(jnp.float32) + got
+            return carry
+
+        lax.fori_loop(0, self.width // WIDE, tile, 0)
+        self.save("middle").start()
+
+    def norm_two(self):
+        for b in range(self.slots):
+            rows = pl.ds(b * self.length, self.length)
+            middle = self.middle_v[rows, :]
+            scale = lax.rsqrt(jnp.mean(middle * middle, axis=-1, keepdims=True) + eps)
+            normed = (middle * scale * self.gain_v[1:2, :]).astype(jnp.bfloat16)
+            self.two_v[rows, :] = normed
+            self.two_t_v[:, rows] = normed.T
+        self.save("two_t").start()
+
+    def hidden(self, part):
+        lo, hi = part
+        self.load("G", part).wait()
+        self.load("U", part).wait()
+        two = self.two_v[...]
+
+        def tile(n, carry):
+            at = pl.multiple_of(lo + n * WIDE, WIDE)
+            cols = pl.ds(at, WIDE)
+            gate = dot(two, self.weight("G", cols))
+            upward = dot(two, self.weight("U", cols))
+            sig = 1.0 / (1.0 + jnp.exp(-gate))
+            silu = gate * sig
+            low = (silu * upward).astype(jnp.bfloat16)
+            self.hid_v[:, cols] = low
+            self.hid_t_v[cols, :] = low.T
+            self.t1_v[:, cols] = (upward * sig * (1.0 + gate * (1.0 - sig))).astype(jnp.bfloat16)
+            self.t2_v[:, cols] = silu.astype(jnp.bfloat16)
+            return carry
+
+        lax.fori_loop(0, (hi - lo) // WIDE, tile, 0)
+
+    def hidden_saves(self):
+        for name in ("hid", "hid_t", "t1", "t2"):
+            self.save(name).start()
+
+    def finish(self):
+        for name in self.save_slots:
+            self.save(name).wait()
+
+
+def split_pair(values):
+    first = iota(values.shape, 1) < HD
+    zero = jnp.zeros_like(values)
+    return jnp.concatenate([jnp.where(first, values, zero), jnp.where(first, zero, values)], axis=0)
+
+
+GATHER_JOBS = (
+    ("D", "rz", (0, 256), (0, 6, 12, 18, 24, 30, 36)),
+    ("g", "zr", None, (1, 4, 7, 10, 14, 18, 20)),
+    ("q", "zr", None, (2, 5, 8, 11, 17, 22, 25)),
+    ("k", "zr", None, (3, 8, 12, 16, 24, 30, 32)),
+    ("v", "zr", None, (6, 12, 17, 22, 31, 37, 40)),
+    ("o", "zr", None, (13, 18, 23, 29, 38, 46, 49)),
+    ("G", "zr", (0, 1536), (18, 23, 29, 36, 47, 56, 60)),
+    ("D", "rz", (256, 512), (24, 33, 40, 48, 57, 66, 75)),
+    ("U", "zr", (0, 1536), (30, 36, 42, 50, 61, 70, 74)),
+    ("G", "zr", (1536, 2816), (40, 46, 52, 63, 74, 83, 87)),
+    ("U", "zr", (1536, 2816), (50, 56, 62, 76, 87, 96, 100)),
+)
+FORWARD_STEPS = (
+    ("tables", (), 2.5),
+    ("live", (), 2.6),
+    ("gains", (), 20.5),
+    ("norm_one", (), 20.6),
+    ("load", ("q",), 25.1),
+    ("project", ("q",), 25.2),
+    ("load", ("k",), 32.1),
+    ("project", ("k",), 32.2),
+    ("load", ("v",), 40.1),
+    ("project", ("v",), 40.2),
+    ("attend", (0,), 45),
+    ("attend", (1,), 48.5),
+    ("load", ("o",), 49.2),
+    ("attend", (2,), 52),
+    ("attend", (3,), 55),
+    ("join", (), 58),
+    ("norm_two", (), 62),
+    ("load", ("G", (0, 1536)), 60.1),
+    ("load", ("U", (0, 1536)), 74.1),
+    ("hidden", ((0, 1536),), 75.5),
+    ("load", ("G", (1536, 2816)), 87.1),
+    ("load", ("U", (1536, 2816)), 100.1),
+    ("hidden", ((1536, 2816),), 100.2),
+    ("hidden_saves", (), 100.3),
+)
+OWNS = ("g", "q", "k", "v", "o", "G", "U", "D")
+SAVED = (
+    "cos", "sin", "normed_t", "q_rot", "k_rot", "v_low", "first", "probs",
+    "mixed_t", "middle", "two_t", "hid", "hid_t", "t1", "t2",
+)
+
+
+def forward_kernel(depth, *refs):
+    refs = list(refs)
+
+    def take(names):
+        return {name: refs.pop(0) for name in names}
+
+    plain = take(("tokens", "counts", "segments", "positions", "inverse"))
+    owns = take(OWNS)
+    fulls = take([n + "_full" for n in OWNS])
+    outs = take([n + "_out" for n in SAVED])
+    held = take([n + "_v" for n in SAVED])
+    weights = take([n + "_v" for n in OWNS[:-1]])
+    rest = take(("gain_v", "normed_v", "mixed_v", "two_v", "bias_v", "live_v"))
+    sems = take(("gather_sems", "load_sems", "save_sems"))
     place = Place(depth)
+    work = Forward(place, {**plain, **fulls, **outs, **held, **weights, **rest, **sems})
+    work.width = held["middle_v"].shape[1]
+    loads = [(args[0], args[1] if len(args) > 1 else None) for name, args, _ in FORWARD_STEPS if name == "load"]
+    work.load_slots = {key: 1 + i for i, key in enumerate(loads)}
+    work.save_slots = {name: i for i, name in enumerate(SAVED)}
+    order = []
+    for i, (name, way, cols, times) in enumerate(GATHER_JOBS):
+        own, full = owns[name], fulls[name + "_full"]
+        wide = full.shape[-1]
+        if cols is not None:
+            own, full = own.at[:, cols[0] : cols[1]], full.at[:, :, :, :, :, cols[0] : cols[1]]
+            wide = cols[1] - cols[0]
+        job = Gather(place, own, full, sems["gather_sems"].at[i], way)
+        job.wide = wide
+        order += list(zip(times, job.steps()))
+
+    def step(name, args):
+        if name == "load":
+            return lambda: work.load(*args).start()
+        return lambda: getattr(work, name)(*args)
+
+    order += [(time, step(name, args)) for name, args, time in FORWARD_STEPS]
     place.greet()
-    jobs = [
-        Gather(place, owns[i], fulls[i], sems.at[i], GATHER_ORDERS[i]).steps() for i in range(count)
-    ]
-    stages = len(jobs[0])
-    for tick in range(count + stages - 1):
-        for stage in reversed(range(stages)):
-            if 0 <= tick - stage < count:
-                jobs[tick - stage][stage]()
-
-
-def gather_all(mesh, shards_in):
+    for _, action in sorted(order, key=lambda e: e[0]):
+        action()
+    work.finish()
+
+
+def forward(mesh, tokens, counts, segments, positions, owns):
     depth = mesh.shape["fsdp"] // 2
-    count = len(shards_in)
-    return pl.pallas_call(
-        lambda *refs: gather_kernel(depth, count, *refs),
-        out_shape=tuple(
-            jax.ShapeDtypeStruct((2, 2, depth, 2) + s.shape, s.dtype) for s in shards_in
+    slots, length, width = tokens.shape
+    rows, low, full = slots * length, jnp.bfloat16, jnp.float32
+    hidden = owns["G"].shape[1]
+    lead = (2, 2, depth, 2)
+    saved = {
+        "cos": ((rows, 128), full),
+        "sin": ((rows, 128), full),
+        "normed_t": ((width, rows), low),
+        "q_rot": ((rows, width), low),
+        "k_rot": ((rows, width), low),
+        "v_low": ((rows, width), low),
+        "first": ((rows, width), low),
+        "probs": ((slots, width // 128, length, 2 * length), low),
+        "mixed_t": ((width, rows), low),
+        "middle": ((rows, width), full),
+        "two_t": ((width, rows), low),
+        "hid": ((rows, hidden), low),
+        "hid_t": ((hidden, rows), low),
+        "t1": ((rows, hidden), low),
+        "t2": ((rows, hidden), low),
+    }
+    inverse = jnp.asarray(
+        np.exp((np.arange(128) % (HD // 2)) * (-2.0 * math.log(10000.0) / HD)), jnp.float32
+    )[None, :]
+    vmem, anywhere = pl.BlockSpec(memory_space=pltpu.VMEM), pl.BlockSpec(memory_space=pl.ANY)
+    smem = pl.BlockSpec(memory_space=pltpu.SMEM)
+    fulls = [jax.ShapeDtypeStruct(lead + owns[n].shape, owns[n].dtype) for n in OWNS]
+    outs = [jax.ShapeDtypeStruct(*saved[n]) for n in SAVED]
+    got = pl.pallas_call(
+        lambda *refs: forward_kernel(depth, *refs),
+        out_shape=tuple(fulls + outs),
+        in_specs=[vmem, smem, vmem, vmem, vmem] + [anywhere] * len(OWNS),
+        out_specs=tuple([anywhere] * (len(OWNS) + len(SAVED))),
+        scratch_shapes=[pltpu.VMEM(*saved[n]) for n in SAVED]
+        + [pltpu.VMEM(lead + owns[n].shape, owns[n].dtype) for n in OWNS[:-1]]
+        + [
+            pltpu.VMEM((8, width), full),
+            pltpu.VMEM((rows, width), low),
+            pltpu.VMEM((rows, width), low),
+            pltpu.VMEM((rows, width), low),
+            pltpu.VMEM((slots, length, length), full),
+            pltpu.VMEM((rows, 128), full),
+            pltpu.SemaphoreType.DMA((len(GATHER_JOBS), 2, 24)),
+            pltpu.SemaphoreType.DMA((16,)),
+            pltpu.SemaphoreType.DMA((len(SAVED),)),
+        ],
+        compiler_params=pltpu.CompilerParams(
+            collective_id=1, has_side_effects=True, vmem_limit_bytes=60 * 2**20
         ),
-        in_specs=[pl.BlockSpec(memory_space=pl.ANY)] * count,
-        out_specs=tuple([pl.BlockSpec(memory_space=pl.ANY)] * count),
-        scratch_shapes=[pltpu.SemaphoreType.DMA((count, 2, 24))],
-        compiler_params=pltpu.CompilerParams(collective_id=1, has_side_effects=True),
-        name="gather_weights",
-    )(*shards_in)
+        cost_estimate=pl.CostEstimate(
+            flops=2 * rows * width * (4 * width + 2 * hidden), bytes_accessed=80 * 2**20, transcendentals=2**22
+        ),
+        name="gather_and_forward",
+    )(tokens.reshape(rows, width), counts, segments, positions, inverse, *[owns[n] for n in OWNS])
+    names = [n + "_full" for n in OWNS] + list(SAVED)
+    return dict(zip(names, got))
 
 
 class Reduce:
@@ -695,25 +1022,6 @@
     return tuple(lax.psum_scatter(t, BOTH, scatter_dimension=0, tiled=True) for t in terms)
 
 
-def linked_gather(mesh):
-    def gather(gain_one, gain_two, *weights):
-        down = weights[-1]
-        rows, wide = down.shape
-        gains = jnp.zeros((8, 128), jnp.float32)
-        gains = gains.at[0, : gain_one.shape[0]].set(gain_one.astype(jnp.float32))
-        gains = gains.at[1, : gain_two.shape[0]].set(gain_two.astype(jnp.float32))
-        down = down.reshape(rows, 2, wide // 2).transpose(1, 0, 2).reshape(2 * rows, wide // 2)
-        fulls = gather_all(mesh, (gains,) + weights[:-1] + (down,))
-        gains_full = fulls[0].reshape(-1, 8, 128)
-        ones = gains_full[:, 0, : gain_one.shape[0]].reshape(-1).astype(jnp.bfloat16)
-        twos = gains_full[:, 1, : gain_two.shape[0]].reshape(-1).astype(jnp.bfloat16)
-        whole = [f.reshape(-1, f.shape[-1]) for f in fulls[1:-1]]
-        down = fulls[-1].reshape(-1, 2, rows, wide // 2).transpose(0, 2, 1, 3)
-        return (ones, twos) + tuple(whole) + (down.reshape(-1, wide),)
-
-    return gather
-
-
 def linked_reduce(mesh):
     lead = (2, 2, mesh.shape["fsdp"] // 2, 2)
     count = mesh.size
@@ -735,6 +1043,196 @@
     return reduce
 
 
+def linked_layer(
+    mesh,
+    tokens,
+    seq_counts,
+    segments,
+    positions,
+    norm_first,
+    query_weight,
+    key_weight,
+    value_weight,
+    output_weight,
+    norm_second,
+    gate_weight,
+    up_weight,
+    down_weight,
+    out_cotangent,
+    value_cotangent,
+):
+    slot_count, seq_length, model_width = tokens.shape
+    row_count = slot_count * seq_length
+    head_count = model_width // HD
+    rows, wide = down_weight.shape
+    gains = jnp.zeros((8, 128), jnp.float32)
+    gains = gains.at[0].set(jnp.tile(norm_first.astype(jnp.float32), 128 // norm_first.shape[0]))
+    gains = gains.at[1].set(jnp.tile(norm_second.astype(jnp.float32), 128 // norm_second.shape[0]))
+    owns = {
+        "g": gains,
+        "q": query_weight,
+        "k": key_weight,
+        "v": value_weight,
+        "o": output_weight,
+        "G": gate_weight,
+        "U": up_weight,
+        "D": down_weight.reshape(rows, 2, wide // 2).transpose(1, 0, 2).reshape(2 * rows, wide // 2),
+    }
+    got = forward(mesh, tokens, seq_counts, segments, positions, owns)
+    whole = [got[n + "_full"].reshape(model_width, -1) for n in "qkvoGU"]
+    query_full, key_full, value_full, output_full, gate_full, up_full = whole
+    down_full = got["D_full"].reshape(-1, 2, rows, wide // 2).transpose(0, 2, 1, 3).reshape(-1, wide)
+    gains_full = got["g_full"].reshape(-1, 8, 128)
+    gain_one = gains_full[:, 0, : norm_first.shape[0]].reshape(-1)
+    gain_two = gains_full[:, 1, : norm_first.shape[0]].reshape(-1)
+    row_index = jnp.arange(row_count, dtype=jnp.int32)
+    slot_index = row_index // seq_length
+    live_rows = (slot_index < seq_counts[0]).astype(jnp.float32)[:, None]
+    flat_segments = segments.reshape(row_count)
+    allowed = (
+        (slot_index[:, None] == slot_index[None, :])
+        & (flat_segments[:, None] == flat_segments[None, :])
+        & (row_index[:, None] >= row_index[None, :])
+    )
+    inputs_f = tokens.reshape(row_count, model_width).astype(jnp.float32)
+    scale_one = rms_scale(inputs_f)
+    cosine, sines = rotate_table(positions.reshape(row_count))
+
+    def rotated(values_in, turn_sign):
+        turned = apply_rotary(
+            values_in.reshape(row_count, head_count, HD), cosine, turn_sign * sines
+        )
+        return turned.reshape(row_count, model_width).astype(jnp.bfloat16)
+
+    normed = got["normed_t"].T
+    query_rot, key_rot, value_low = got["q_rot"], got["k_rot"], got["v_low"]
+    query_groups = stack_groups(query_rot)
+    key_groups = stack_groups(key_rot)
+    value_groups = stack_groups(value_low)
+    mixed_low = got["mixed_t"].T
+    middle = got["middle"]
+    scale_two = rms_scale(middle)
+    normed_two = got["two_t"].T
+    hidden = got["hid"]
+    block_out = (live_rows * (middle + matmul(hidden, down_full))).astype(jnp.bfloat16)
+    first_values = got["first"]
+    probs = got["probs"].reshape(slot_count, model_width // 256, 2, seq_length, 2, seq_length)
+    probs = probs.transpose(1, 2, 4, 0, 3, 5).reshape(model_width // 256, 4, slot_count, seq_length, seq_length)
+    spread = jnp.zeros((model_width // 256, 4, slot_count, seq_length, slot_count, seq_length), jnp.bfloat16)
+    for s in range(slot_count):
+        spread = spread.at[:, :, s, :, s].set(probs[:, :, s])
+    probs = spread.reshape(model_width // 256, 4, row_count, row_count)
+    reduce_set = linked_reduce(mesh)
+    grad_y = live_rows * out_cotangent.reshape(row_count, model_width).astype(jnp.float32)
+    grad_branch = grad_y.astype(jnp.bfloat16)
+    down_term = jnp.einsum("rf,rd->fd", hidden, grad_branch, preferred_element_type=jnp.float32)
+    grad_hidden = jnp.einsum(
+        "rd,fd->rf", grad_branch, down_full, preferred_element_type=jnp.float32
+    )
+    grad_gate = (
+        grad_hidden * got["t1"].astype(jnp.float32)
+    ).astype(jnp.bfloat16)
+    grad_up = (grad_hidden * got["t2"].astype(jnp.float32)).astype(jnp.bfloat16)
+    gate_term = jnp.einsum("rd,rf->df", normed_two, grad_gate, preferred_element_type=jnp.float32)
+    up_term = jnp.einsum("rd,rf->df", normed_two, grad_up, preferred_element_type=jnp.float32)
+    grad_normed_two = jnp.einsum(
+        "rf,df->rd", grad_gate, gate_full, preferred_element_type=jnp.float32
+    ) + jnp.einsum("rf,df->rd", grad_up, up_full, preferred_element_type=jnp.float32)
+    grad_middle_norm, gain_two_term = norm_back(
+        grad_normed_two, middle, scale_two, gain_two.astype(jnp.float32)
+    )
+    grad_middle = grad_y + grad_middle_norm
+    grad_attended = grad_middle.astype(jnp.bfloat16)
+    output_term = jnp.einsum(
+        "rd,re->de", mixed_low, grad_attended, preferred_element_type=jnp.float32
+    )
+    grad_mixed = jnp.einsum(
+        "re,de->rd", grad_attended, output_full, preferred_element_type=jnp.float32
+    ).astype(jnp.bfloat16)
+
+    def attend_back(operands):
+        query_grp, key_grp, value_grp, grad_grp, probs_low = operands
+        probs_full = probs_low.astype(jnp.float32)
+        grad_heads = grad_grp.reshape(row_count, 4, HD)
+        value_heads = value_grp.reshape(row_count, 4, HD)
+        query_heads = query_grp.reshape(row_count, 4, HD)
+        key_heads = key_grp.reshape(row_count, 4, HD)
+        grad_probs = jnp.einsum(
+            "qhe,khe->hqk", grad_heads, value_heads, preferred_element_type=jnp.float32
+        )
+        row_term = jnp.sum(probs_full * grad_probs, axis=-1, keepdims=True)
+        grad_scores = (probs_full * (grad_probs - row_term)).astype(jnp.bfloat16)
+        score_scale = HD ** (-0.5)
+        grad_query = (
+            jnp.einsum("hqk,khe->qhe", grad_scores, key_heads, preferred_element_type=jnp.float32)
+            * score_scale
+        )
+        grad_key = (
+            jnp.einsum("hqk,qhe->khe", grad_scores, query_heads, preferred_element_type=jnp.float32)
+            * score_scale
+        )
+        grad_value = jnp.einsum(
+            "hqk,qhe->khe", probs_low, grad_heads, preferred_element_type=jnp.float32
+        )
+        group_width = 4 * HD
+        return (
+            grad_query.reshape(row_count, group_width),
+            grad_key.reshape(row_count, group_width),
+            grad_value.reshape(row_count, group_width),
+        )
+
+    grad_q_groups, grad_k_groups, grad_v_groups = lax.map(
+        attend_back, (query_groups, key_groups, value_groups, stack_groups(grad_mixed), probs)
+    )
+    grad_query = rotated(unstack_groups(grad_q_groups), -1.0)
+    grad_key = rotated(unstack_groups(grad_k_groups), -1.0)
+    grad_value = (
+        unstack_groups(grad_v_groups)
+        + live_rows * value_cotangent.reshape(row_count, model_width).astype(jnp.float32)
+    ).astype(jnp.bfloat16)
+    query_term = jnp.einsum("rd,re->de", normed, grad_query, preferred_element_type=jnp.float32)
+    key_term = jnp.einsum("rd,re->de", normed, grad_key, preferred_element_type=jnp.float32)
+    value_term = jnp.einsum("rd,re->de", normed, grad_value, preferred_element_type=jnp.float32)
+    grad_normed = jnp.einsum(
+        "re,de->rd", grad_query, query_full, preferred_element_type=jnp.float32
+    )
+    grad_normed = grad_normed + jnp.einsum(
+        "re,de->rd", grad_key, key_full, preferred_element_type=jnp.float32
+    )
+    grad_normed = grad_normed + jnp.einsum(
+        "re,de->rd", grad_value, value_full, preferred_element_type=jnp.float32
+    )
+    grad_inputs_norm, gain_one_term = norm_back(
+        grad_normed, inputs_f, scale_one, gain_one.astype(jnp.float32)
+    )
+    token_grad = (grad_middle + grad_inputs_norm).astype(jnp.bfloat16).reshape(tokens.shape)
+    grads = reduce_set(
+        gain_one_term,
+        gain_two_term,
+        query_term,
+        key_term,
+        value_term,
+        output_term,
+        gate_term,
+        up_term,
+        down_term,
+    )
+    return (
+        block_out.reshape(tokens.shape),
+        first_values.reshape(tokens.shape),
+        token_grad,
+        grads[0],
+        grads[2],
+        grads[3],
+        grads[4],
+        grads[5],
+        grads[1],
+        grads[6],
+        grads[7],
+        grads[8],
+    )
+
+
 def solution(mesh):
     in_specs = (
         P(("dp", "fsdp"), None, None),
@@ -768,11 +1266,11 @@
         P(("dp", "fsdp"), None),
     )
     if dict(mesh.shape) == {"dp": 4, "fsdp": 8}:
-        sets = (linked_gather(mesh), linked_reduce(mesh))
+        whole_layer = lambda *args: linked_layer(mesh, *args)
     else:
-        sets = (plain_gather, plain_reduce)
+        whole_layer = lambda *args: layer(plain_gather, plain_reduce, *args)
 
     def shards(*args):
-        return layer(*sets, *args)
+        return whole_layer(*args)
 
     return jax.shard_map(shards, mesh=mesh, in_specs=in_specs, out_specs=out_specs, check_vma=False)

time: 517 us -> 513 us (level)
  matrix products: 113 us -> 76.4 us
  local copies, waits for them, and re-layouts: 96.9 us -> 129 us
  other arithmetic: 26.9 us -> 13.8 us
  Pallas kernels: 273 us -> 282 us
    while x0 -> x10, local copies, waits for them, and re-layouts: none -> 26.8 us  [the longest x2 26.8 us: linked_layer(): lax.map(attend_back, (query_groups, key_groups, value_groups, stack_group...]
    dot_general x7 -> x1, matrix products: 29.3 us -> 4.13 us  [matmul(): return jnp.dot(left_arg, right_arg, preferred_element_type=jnp.float32)]
    dot_general x26 -> x14, matrix products: 67.7 us -> 55 us  [the longest x1 7.19 us: linked_layer(): jnp.einsum('rf,df->rd', grad_gate, gate_full, preferred_element_type=jnp....]
    dot_general x2 -> x0, local copies, waits for them, and re-layouts: 8 us -> none  [matmul(): return jnp.dot(left_arg, right_arg, preferred_element_type=jnp.float32)]
    scatter x1 -> x6, local copies, waits for them, and re-layouts: 0.09 us -> 8.04 us  [the longest x4 8.01 us: linked_layer(): spread = spread.at[:, :, s, :, s].set(probs[:, :, s])]
    reshape x2 -> x5, local copies, waits for them, and re-layouts: 11.1 us -> 18.5 us  [the longest x1 8.87 us: linked_layer(): got['D_full'].reshape(-1, 2, rows, wide // 2).transpose(0, 2, 1, 3)]
    reshape x2 -> x4, local copies, waits for them, and re-layouts: 2.06 us -> 9.15 us  [stack_groups(): values_in.reshape(row_count, model_width // (4 * HD), 4 * HD)]
    unnamed x99 -> x92, local copies, waits for them, and re-layouts: 17.1 us -> 11.5 us
where the time goes in v2:
time: 513 us; the launch traced here: 503 us
  Pallas kernels  282 us (55%)
  local copies, waits for them, and re-layouts  129 us (25%)
  matrix products  76.4 us (15%)
  other arithmetic  13.8 us (3%)
    pallas_call x1, Pallas kernels, forward(): pl.pallas_call(lambda *refs: forward_kernel(depth, *refs), out_shape=tupl...  142 us
    pallas_call x1, Pallas kernels, reduce_all(): pl.pallas_call(lambda *refs: reduce_kernel(depth, count, *refs), out_shap...  140 us
    while x2, local copies, waits for them, and re-layouts, linked_layer(): lax.map(attend_back, (query_groups, key_groups, value_groups, stack_group...  26.8 us
    dynamic_slice x16, local copies, waits for them, and re-layouts, linked_layer(): lax.map(attend_back, (query_groups, key_groups, value_groups, stack_group...  17.9 us
    reshape x2, local copies, waits for them, and re-layouts, reduce(): down = low[-1].reshape(count, rows, 2, wide // 2).transpose(0, 2, 1, 3)  17 us
    unnamed x92, local copies, waits for them, and re-layouts  11.5 us

profile of v2, /device:TPU:0, one launch (start us, length us, event | category | flops | bytes accessed | tf_op | source)
XLA Modules:
  0.0 503.3 jit_solution(16208800475161790247)
XLA Ops:
  2.8 1.6 copy.86
  4.4 142.1 %gather_and_forward.1 = (f32[2,2,4,2,8,128]{5,4,3,2,1,0:T(8,128)}, bf16[2,2,4,2,32,1024]{5,4,3,2,1,0:T(8,128)(2,1)}, bf16[2,2,4,2,32,1024]{5,4,3,2,1,0:T(8,128)(...) custom-call(bf16[512,1024]{1,0:T(8,128)(2,1)} %bitcast.206, ...), custom_call_target="tpu_custom_call" | custom-call | flops 10200547328 | bytes 83886080 | tf_op jit(solution)/shard_map/gather_and_forward/pallas_call | solution.py:545
  146.5 8.9 %copy.59 = bf16[32,2,88,512]{3,1,2,0:T(2,128)(2,1)S(1)} copy(bf16[32,2,88,512]{3,2,1,0:T(8,128)(2,1)} %bitcast.212) | data formatting | bytes 11534336 | tf_op jit(solution)/shard_map/reshape | solution.py:1084
  155.4 1.9 copy.84
  157.8 4.1 multiply_convert_fusion.3
  163.7 6.0 %fusion.34 = f32[512,2816]{1,0:T(8,128)S(1)} fusion(bf16[512,1024]{1,0:T(8,128)(2,1)S(1)} %bitcast.229, bf16[2816,1024]{1,0:T(8,128)(2,1)} %bitcast.214), kind=kOutput, calls=%fused_computation.101 | convolution fusion | flops 2952790016 | bytes 12582912 | tf_op jit(solution)/shard_map/rd,fd->rf/dot_general | solution.py:1129
  169.7 7.2 %fusion.33 = f32[512,1024]{1,0:T(8,128)S(1)} fusion(bf16[1024,2816]{1,0:T(8,128)(2,1)S(1)} %bitcast.247, f32[512,2816]{1,0:T(8,128)S(1)} %fusion.34, bf16[512,2816]{1,0:T(8,128)(2,1)} %get-tuple-element.189), kind=kOutput, calls=%fused_computation.100 | convolution fusion | flops 2957115392 | bytes 16515072 | tf_op jit(solution)/shard_map/rf,df->rd/dot_general | solution.py:1138
  177.0 5.5 %multiply_reduce_fusion = (f32[1024]{0:T(1024)S(1)}, f32[512]{0:T(512)S(1)}, f32[512,1024]{1,0:T(8,128)S(1)}) fusion(f32[512,1024]{1,0:T(8,128)S(1)} %copy-done.4, f32[512]{0:T(512)S(1)} %add_rsqrt_fusion, f32[1024]{0:T(1024)S(1)} %mul.260, f32[512,1024]{1,0:T(8,128)S(1)} %fusion.33, bf16[1024,2816]{1,0:T(8,128)(2,1)S(1)} %bitcast.244, ...), kind=kOutput, calls=%fused_computation.42 | convolution fusion | flops 2960783872 | bytes 20721664 | tf_op jit(solution)/shard_map/rf,df->rd/dot_general | solution.py:1140
  182.5 2.7 fusion.18
  185.6 2.3 copy.74
  187.9 3.9 reshape.639
  191.8 2.1 copy.61
  194.0 5.5 %scatter.30 = bf16[4,4,4,128,4,128]{5,3,1,0,4,2:T(8,128)(2,1)} pad(bf16[4,4,1,128,1,128]{5,3,1,0,4,2:T(8,128)(2,1)S(1)} %slice_bitcast_fusion.3, bf16[]{:T(256)} %constant.285.clone.1), padding=0_0x0_0x0_3x0_0x0_3x0_0 | pad | bytes 8912898 | tf_op jit(solution)/shard_map/scatter | solution.py:1123
  202.0 13.7 %copy.75 = bf16[4,4,4,128,4,128]{3,2,5,4,1,0:T(4,128)(2,1)} copy(bf16[4,4,4,128,4,128]{5,3,1,0,4,2:T(8,128)(2,1)} %fusion.19) | data formatting | bytes 16777216 | tf_op jit(solution)/shard_map/while | solution.py:1184
  215.7 13.1 %reshape.671 = bf16[4,4,512,512]{2,3,1,0:T(8,128)(2,1)} reshape(bf16[4,4,4,128,4,128]{3,2,5,4,1,0:T(4,128)(2,1)} %copy.75) | data formatting | bytes 16777216 | tf_op jit(solution)/shard_map/while | solution.py:1184
  228.8 4.5 convolution_convert_fusion.7
  233.3 2.3 copy.76
  235.5 2.3 copy.77
  237.8 2.3 copy.78
  240.1 45.5 %while.22 = (s32[]{:T(128)}, f32[4,512,256]{1,2,0:T(8,128)}, f32[4,512,256]{1,2,0:T(8,128)}, f32[4,512,256]{1,2,0:T(8,128)S(1)}, bf16[4,512,256]{1,2,0:T(8,128)(...) while((s32[]{:T(128)}, f32[4,512,256]{1,2,0:T(8,128)}, ...), condition=%wide.region_5.6_spmd, body=%wide.region_3.5_spmd.sunk | while | flops 544471040 | bytes 62668972 | solution.py:1184
  242.4 1.2 constant_dynamic-slice_fusion.10
  243.6 2.4 fusion.87
  253.9 1.2 constant_dynamic-slice_fusion.10
  255.0 2.4 fusion.87
  266.4 2.4 fusion.87
  277.8 2.4 fusion.87
  285.6 3.0 reshape.672
  288.6 3.3 copy.79
  291.9 2.3 fusion.17
  295.6 2.2 copy-done.27
  297.8 1.3 fusion.35
  299.4 1.3 fusion.36
  301.0 2.0 fusion.14
  303.0 1.7 fusion.11
  305.5 4.3 convolution_convert_fusion.6
  309.8 2.6 convolution_convert_fusion.5
  312.4 2.0 copy.80
  314.4 2.0 fusion.16
  316.4 2.6 convolution_convert_fusion.4
  319.0 2.7 convolution_convert_fusion.3
  322.8 5.0 convolution_convert_fusion.2
  327.8 5.0 convolution_convert_fusion.1
  332.8 5.1 %convolution_convert_fusion = bf16[2816,1024]{1,0:T(8,128)(2,1)} fusion(bf16[512,2816]{1,0:T(8,128)(2,1)S(1)} %copy-done.36, bf16[512,1024]{1,0:T(8,128)(2,1)S(1)} %copy-done.16), kind=kOutput, calls=%fused_computation.19 | convolution fusion | flops 2955673600 | bytes 9699328 | tf_op jit(solution)/shard_map/rf,rd->fd/dot_general | solution.py:1128
  337.9 10.5 %reshape.664 = bf16[32,88,2,512]{3,2,1,0:T(2,128)(2,1)} reshape(bf16[2816,1024]{1,0:T(8,128)(2,1)} %convolution_convert_fusion) | data formatting | bytes 11534336 | tf_op jit(solution)/shard_map/reshape | solution.py:1037
  348.4 6.5 %copy.69 = bf16[32,88,2,512]{3,1,2,0:T(8,128)(2,1)} copy(bf16[32,88,2,512]{3,2,1,0:T(2,128)(2,1)} %reshape.664) | data formatting | bytes 11534336 | tf_op jit(solution)/shard_map/reshape | solution.py:1037
  354.9 140.1 %reduce_grads.1 = (f32[8,128]{1,0:T(8,128)}, f32[32,1024]{1,0:T(8,128)}, f32[32,1024]{1,0:T(8,128)}, f32[32,1024]{1,0:T(8,128)}, f32[32,1024]{1,0:T(8,128)}, /*i...) custom-call(f32[2,2,4,2,8,128]{5,4,3,2,1,0:T(8,128)} %bitcast.236, ...), custom_call_target="tpu_custom_call" | custom-call | tf_op jit(solution)/shard_map/reduce_grads/pallas_call | solution.py:749
  495.0 1.3 slice_bitcast_fusion.4
  496.3 1.7 copy.83
  (173 shorter events, 49.1 us)
Async XLA Ops:
  2.8 1.6 copy-start.24
  155.4 2.0 copy-start.4
  155.4 2.4 copy-start.35
  157.3 4.6 copy-start.5
  162.0 1.5 copy-start.7
  163.4 6.3 %slice-start.2 = ((s8[5767168]{0:T(1024)(128)(4,1)}), s8[4194304]{0:T(1024)(128)(4,1)S(1)}, s32[]{:S(2)}) async-start(s8[5767168]{0:T(1024)(128)(4,1)} %bitcast.245), calls=%async_computation.2 | async-start | bytes 8388608
  163.7 6.0 %slice-start.3 = ((s8[5767168]{0:T(1024)(128)(4,1)}), s8[1572864]{0:T(1024)(128)(4,1)S(1)}, s32[]{:S(2)}) async-start(s8[5767168]{0:T(1024)(128)(4,1)} %bitcast.245), calls=%async_computation.3 | async-start | bytes 3145728
  163.7 13.2 %slice-start = ((s8[5767168]{0:T(1024)(128)(4,1)}), s8[4194304]{0:T(1024)(128)(4,1)S(1)}, s32[]{:S(2)}) async-start(s8[5767168]{0:T(1024)(128)(4,1)} %bitcast.242), calls=%async_computation | async-start | bytes 8388608
  169.7 7.2 %copy-start.28 = (f32[512,2816]{1,0:T(8,128)}, f32[512,2816]{1,0:T(8,128)S(1)}, u32[]{:S(2)}) copy-start(f32[512,2816]{1,0:T(8,128)S(1)} %fusion.34) | copy-start | bytes 17301508
  169.7 7.2 %slice-start.1 = ((s8[5767168]{0:T(1024)(128)(4,1)}), s8[1572864]{0:T(1024)(128)(4,1)S(1)}, s32[]{:S(2)}) async-start(s8[5767168]{0:T(1024)(128)(4,1)} %bitcast.242), calls=%async_computation.1 | async-start | bytes 3145728
  177.0 5.5 %copy-start.8 = (bf16[4,128,1024]{2,1,0:T(8,128)(2,1)S(1)}, bf16[4,128,1024]{2,1,0:T(8,128)(2,1)}, u32[]{:S(2)}) copy-start(bf16[4,128,1024]{2,1,0:T(8,128)(2,1)} %param.47) | copy-start | bytes 3145732
  182.5 2.7 copy-start.1
  240.1 5.9 %copy-start = (bf16[4,4,512,512]{2,3,1,0:T(8,128)(2,1)S(1)}, bf16[4,4,512,512]{2,3,1,0:T(8,128)(2,1)}, u32[]{:S(2)}) copy-start(bf16[4,4,512,512]{2,3,1,0:T(8,128)(2,1)} %get-tuple-element.357) | copy-start | bytes 25165828 | tf_op jit(solution)/shard_map/while
  251.5 5.9 %copy-start = (bf16[4,4,512,512]{2,3,1,0:T(8,128)(2,1)S(1)}, bf16[4,4,512,512]{2,3,1,0:T(8,128)(2,1)}, u32[]{:S(2)}) copy-start(bf16[4,4,512,512]{2,3,1,0:T(8,128)(2,1)} %get-tuple-element.357) | copy-start | bytes 25165828 | tf_op jit(solution)/shard_map/while
  262.9 5.9 %copy-start = (bf16[4,4,512,512]{2,3,1,0:T(8,128)(2,1)S(1)}, bf16[4,4,512,512]{2,3,1,0:T(8,128)(2,1)}, u32[]{:S(2)}) copy-start(bf16[4,4,512,512]{2,3,1,0:T(8,128)(2,1)} %get-tuple-element.357) | copy-start | bytes 25165828 | tf_op jit(solution)/shard_map/while
  274.3 5.9 %copy-start = (bf16[4,4,512,512]{2,3,1,0:T(8,128)(2,1)S(1)}, bf16[4,4,512,512]{2,3,1,0:T(8,128)(2,1)}, u32[]{:S(2)}) copy-start(bf16[4,4,512,512]{2,3,1,0:T(8,128)(2,1)} %get-tuple-element.357) | copy-start | bytes 25165828 | tf_op jit(solution)/shard_map/while
  291.9 2.4 copy-start.25
  291.9 2.7 copy-start.9
  291.9 2.9 copy-start.10
  295.5 2.4 copy-start.27
  295.6 3.5 copy-start.15
  295.6 3.5 copy-start.13
  297.8 1.6 copy-start.26
  299.4 1.6 copy-start.11
  301.0 2.0 copy-start.2
  305.5 4.3 copy-start.17
  305.5 4.3 copy-start.14
  305.5 4.3 copy-start.33
  312.4 2.0 copy-start.6
  314.4 2.0 copy-start.34
  316.4 2.6 copy-start.3
  316.4 2.6 copy-start.32
  316.4 5.3 %slice-start.4 = ((s8[5767168]{0:T(1024)(128)(4,1)}), s8[4194304]{0:T(1024)(128)(4,1)S(1)}, s32[]{:S(2)}) async-start(s8[5767168]{0:T(1024)(128)(4,1)} %bitcast.252), calls=%async_computation.4 | async-start | bytes 8388608
  319.0 2.7 slice-start.5
  319.0 3.4 copy-start.30
  319.0 3.7 copy-start.31
  322.8 5.0 copy-start.29
  327.7 5.0 %copy-start.16 = (bf16[512,1024]{1,0:T(8,128)(2,1)S(1)}, bf16[512,1024]{1,0:T(8,128)(2,1)}, u32[]{:S(2)}) copy-start(bf16[512,1024]{1,0:T(8,128)(2,1)} %get-tuple-element.257) | copy-start | bytes 3145732
  327.7 5.0 %copy-start.36 = (bf16[512,2816]{1,0:T(8,128)(2,1)S(1)}, bf16[512,2816]{1,0:T(8,128)(2,1)}, u32[]{:S(2)}) copy-start(bf16[512,2816]{1,0:T(8,128)(2,1)} %get-tuple-element.186) | copy-start | bytes 8650756
  354.9 143.2 %copy-start.12 = (bf16[512,1024]{1,0:T(8,128)(2,1)S(1)}, bf16[512,1024]{1,0:T(8,128)(2,1)}, u32[]{:S(2)}) copy-start(bf16[512,1024]{1,0:T(8,128)(2,1)} %get-tuple-element.188) | copy-start | bytes 3145732
  495.0 4.0 copy-start.23
  495.0 4.7 copy-start.22
  495.0 5.3 %copy-start.21 = (f32[32,1024]{1,0:T(8,128)S(1)}, f32[32,1024]{1,0:T(8,128)}, u32[]{:S(2)}) copy-start(f32[32,1024]{1,0:T(8,128)} %get-tuple-element.380) | copy-start | bytes 393220
  495.0 6.0 %copy-start.20 = (f32[32,1024]{1,0:T(8,128)S(1)}, f32[32,1024]{1,0:T(8,128)}, u32[]{:S(2)}) copy-start(f32[32,1024]{1,0:T(8,128)} %get-tuple-element.381) | copy-start | bytes 393220
  495.0 6.6 %copy-start.19 = (f32[32,2816]{1,0:T(8,128)S(1)}, f32[32,2816]{1,0:T(8,128)}, u32[]{:S(2)}) copy-start(f32[32,2816]{1,0:T(8,128)} %get-tuple-element.383) | copy-start | bytes 1081348
  498.1 4.3 copy-start.18
